TPU v7x, 32 devices: a whole 2x2x4 slice. The times are simulated.
32 devices in a mesh: outer: 8 (over y, x, core), inner: 4 (over z).
Axes of the slice: x: 2, y: 2, z: 4, core: 2. Of those that a mesh axis runs over, the one named last changes fastest.
Arguments:
- queries: bfloat16 [4096, 2048], P(('outer', 'inner')), may hold values from -6 to 6
- keys: bfloat16 [4096, 2, 2048], P(('outer', 'inner')), may hold values from -6 to 6
- values: bfloat16 [4096, 2, 2048], P(('outer', 'inner')), may hold values from -6 to 6
- beta_logit: float32 [2, 16, 4096], P(None, None, ('outer', 'inner')), may hold values from -1.5 to 11
- gain: float32 [2048], replicated, may hold values from 0.5 to 1.5
Outputs:
- mixed: bfloat16 [4096, 2048], P(('outer', 'inner'))
All inputs are finite; a program needn't handle non-finite values.
Results may differ from a plain program's by a relative error of at most 0.0045.
Values sent between devices are 32-bit elements; how exact they have to be, the bound alone decides.
A program may use at most 64 MiB of HBM per device.

v0:
```python
import jax
import jax.numpy as jnp
from jax import lax
from jax.sharding import PartitionSpec as P

HIGH = lax.Precision.HIGHEST


def passed_along(value, axis, by):
    count = lax.axis_size(axis)
    pairs = [(i, i + by) for i in range(count) if 0 <= i + by < count]
    return lax.ppermute(value, axis, pairs)


def unit_rows(field):
    return field / jnp.sqrt(jnp.sum(field * field, axis=-1, keepdims=True) + 1e-06)


def block_terms(queries, keys, values, logits):
    count = queries.shape[0]
    heads = logits.shape[1]
    size = queries.shape[1] // heads
    rows = 2 * count
    qf = unit_rows(queries.astype(jnp.float32).reshape(count, heads, size).transpose(1, 0, 2))
    kf = unit_rows(
        keys.astype(jnp.float32)
        .reshape(count, 2, heads, size)
        .transpose(2, 0, 1, 3)
        .reshape(heads, rows, size)
    )
    vf = (
        values.astype(jnp.float32)
        .reshape(count, 2, heads, size)
        .transpose(2, 0, 1, 3)
        .reshape(heads, rows, size)
    )
    beta = (2.0 * jax.nn.sigmoid(logits)).transpose(1, 2, 0).reshape(heads, rows)
    gram = jnp.einsum("hrd,hsd->hrs", kf, kf, precision=HIGH)
    row_ids = lax.broadcasted_iota(jnp.int32, (rows, rows), 0)
    col_ids = lax.broadcasted_iota(jnp.int32, (rows, rows), 1)
    strict = (row_ids > col_ids)[None]
    eye_rows = jnp.eye(rows, dtype=jnp.float32)[None]
    system = eye_rows + jnp.where(strict, gram * beta[:, None, :], 0.0)
    both = jnp.concatenate([vf, kf], axis=-1)
    solved = lax.linalg.triangular_solve(
        system, both, left_side=True, lower=True, unit_diagonal=True
    )
    fresh = solved[..., :size]
    wmat = solved[..., size:]
    kscaled = kf * beta[:, :, None]
    trans = jnp.eye(size, dtype=jnp.float32)[None] - jnp.einsum(
        "hrd,hre->hde", kscaled, wmat, precision=HIGH
    )
    offset = jnp.einsum("hrd,hre->hde", kscaled, fresh, precision=HIGH)
    scores = jnp.einsum("htd,hsd->hts", qf, kscaled, precision=HIGH)
    tok_ids = lax.broadcasted_iota(jnp.int32, (count, rows), 0)
    virt_ids = lax.broadcasted_iota(jnp.int32, (count, rows), 1)
    scores = jnp.where((virt_ids <= 2 * tok_ids + 1)[None], scores, 0.0)
    local_out = jnp.einsum("hts,hse->hte", scores, fresh, precision=HIGH)
    carried_q = qf - jnp.einsum("hts,hsd->htd", scores, wmat, precision=HIGH)
    return (trans, offset, local_out, carried_q)


def matmul_heads(left, right):
    return jnp.einsum("hde,hef->hdf", left, right, precision=HIGH)


def compose_group(received):
    maps_a = received[0][:, 0]
    maps_b = received[1][:, 0]
    items = maps_a.shape[1]
    size = maps_a.shape[2]
    eye_maps = jnp.broadcast_to(jnp.eye(size, dtype=jnp.float32), (items, size, size))
    zero_maps = jnp.zeros((items, size, size), jnp.float32)

    def step(carry, piece):
        acc_a, acc_b = carry
        piece_a, piece_b = piece
        updated = (matmul_heads(piece_a, acc_a), matmul_heads(piece_a, acc_b) + piece_b)
        return (updated, carry)

    totals, prefixes = lax.scan(step, (eye_maps, zero_maps), (maps_a, maps_b))
    return (prefixes[0], prefixes[1], totals[0][None], totals[1][None])


def local(queries, keys, values, beta_logit, gain):
    trans, offset, local_out, carried_q = block_terms(queries, keys, values, beta_logit)
    heads, size = (trans.shape[0], trans.shape[1])
    n_inner = lax.axis_size("inner")
    owned = heads // n_inner
    trans_split = trans.reshape(1, n_inner, owned, size, size)
    offset_split = offset.reshape(1, n_inner, owned, size, size)
    pre_a, pre_b, tot_a, tot_b = compose_group(
        (
            lax.all_to_all(trans_split, "inner", split_axis=1, concat_axis=0, tiled=True),
            lax.all_to_all(offset_split, "inner", split_axis=1, concat_axis=0, tiled=True),
        )
    )
    tot_a = tot_a[0]
    tot_b = tot_b[0]
    zero_maps = jnp.zeros((owned, size, size), jnp.float32)
    n_outer = lax.axis_size("outer")

    def advance(index, current):
        return passed_along(matmul_heads(tot_a, current) + tot_b, "outer", 1)

    start = lax.fori_loop(0, n_outer - 1, advance, zero_maps)
    entry = jnp.einsum("ihde,hef->ihdf", pre_a, start, precision=HIGH) + pre_b
    entry = lax.all_to_all(entry, "inner", split_axis=0, concat_axis=1, tiled=True)
    state = entry[0]
    outs = local_out + jnp.einsum("htd,hde->hte", carried_q, state, precision=HIGH)
    scale = jnp.sqrt(jnp.mean(outs * outs, axis=-1, keepdims=True) + 1e-06)
    normed = outs / scale * gain.reshape(heads, 1, size)
    count = queries.shape[0]
    return normed.transpose(1, 0, 2).reshape(count, heads * size).astype(jnp.bfloat16)


def solution(mesh):
    return jax.shard_map(
        local,
        mesh=mesh,
        in_specs=(
            P(("outer", "inner"), None),
            P(("outer", "inner"), None, None),
            P(("outer", "inner"), None, None),
            P(None, None, ("outer", "inner")),
            P(),
        ),
        out_specs=P(("outer", "inner"), None),
        check_vma=False,
    )
```

profile of v0, /device:TPU:6, one launch (start us, length us, event | category | flops | bytes accessed | tf_op | source)
XLA Modules:
  0.0 531.7 jit_solution(15175509296949295681)
XLA Ops:
  0.0 3.7 copy_bitcast_fusion.1
  3.7 2.3 fusion.19
  7.0 2.1 broadcast_divide_fusion
  9.1 5.7 %select_add_fusion = f32[16,256,256]{2,1,0:T(8,128)} fusion(f32[16,256,128]{2,1,0:T(8,128)S(1)} %broadcast_divide_fusion, f32[256,256]{1,0:T(8,128)S(1)} %get-tuple-element.141, f32[16,256]{1,0:T(8,128)S(1)} %copy.91, f32[256,256]{1,0:T(8,128)S(1)} %get-tuple-element.140, pred[256,256]{1,0:T(8,128)(4,1)S(1)} %get-tuple-element.138, ...), kind=kOutput, calls=%fused_computation.22 | convolution fusion | flops 1615855616 | bytes 6963200 | tf_op jit(solution)/shard_map/hrd,hsd->hrs/dot_general | solution.py:38
  14.8 9.2 %while.29 = (s32[]{:T(128)}, f32[16,256,256]{2,1,0:T(8,128)}, s32[2,2]{1,0:T(2,128)S(1)}, f32[2,16,128,128]{3,2,0,1:T(8,128)}, s32[]{:T(128)}) while((s32[]{:T(128)}, f32[16,256,256]{2,1,0:T(8,128)}, s32[2,2]{1,0:T(2,128)S(1)}, f32[2,16,128,128]{3,2,0,1:T(8,128)}, s32[]{:T(128)}) %tuple.52), condition=%wide.while_cond, body=%wide.while_body.sunk | while | flops 2 | bytes 2098785 | solution.py:45
  15.5 4.2 bitcast_dynamic-update-slice_fusion.4
  20.3 3.8 bitcast_dynamic-update-slice_fusion.4
  24.1 315.8 %custom-call.3 = f32[16,2,128,128]{2,3,1,0:T(8,128)} custom-call(f32[16,2,128,128]{3,2,1,0:T(8,128)} %bitcast.133), custom_call_target="InvertDiagBlocksLowerTriangular" | custom-call | tf_op jit(solution)/shard_map/triangular_solve | solution.py:45
  343.5 4.0 fusion.40
  347.5 2.2 fusion.16
  349.7 5.5 %fusion.24 = f32[16,128,128]{2,1,0:T(8,128)} fusion(f32[16,256,128]{2,1,0:T(8,128)S(1)} %broadcast_divide_fusion, f32[16,256]{1,0:T(8,128)S(1)} %copy.91, f32[16,128,256]{2,1,0:T(8,128)S(1)} %fusion.13, f32[16,128,256]{2,1,0:T(8,128)S(1)} %fusion.16), kind=kOutput, calls=%fused_computation.41 | convolution fusion | flops 806354944 | bytes 7356416 | tf_op jit(solution)/shard_map/hrd,hre->hde/dot_general | solution.py:54
  355.2 4.9 all-to-all-start.1
  360.1 6.8 %fusion.30 = f32[16,128,128]{2,1,0:T(8,128)} fusion(f32[16,256,128]{2,1,0:T(8,128)S(1)} %broadcast_divide_fusion, f32[16,256]{1,0:T(8,128)S(1)} %copy.91, f32[16,128,256]{2,1,0:T(8,128)} %copy-done.3, f32[16,128,256]{2,1,0:T(8,128)} %copy-done, f32[128,128]{1,0:T(8,128)S(1)} %fusion.57), kind=kOutput, calls=%fused_computation.47 | convolution fusion | flops 806617088 | bytes 7421952 | tf_op jit(solution)/shard_map/hrd,hre->hde/dot_general | solution.py:51
  366.9 18.9 %all-to-all-done.1 = f32[1,4,4,128,128]{4,3,2,0,1:T(8,128)S(1)} async-done(((f32[1,4,4,128,128]{4,3,2,0,1:T(8,128)}), f32[1,4,4,128,128]{4,3,2,0,1:T(8,128)S(1)}, u32[]{:S(2)}, u32[]{:S(2)}) %all-to-all-start.1) | async-done | bytes 1048608 | tf_op jit(solution)/shard_map/all_to_all | solution.py:96
  386.7 3.5 all-to-all-start
  390.3 25.2 %all-to-all-done = f32[1,4,4,128,128]{4,3,2,0,1:T(8,128)S(1)} async-done(((f32[1,4,4,128,128]{4,3,2,0,1:T(8,128)}), f32[1,4,4,128,128]{4,3,2,0,1:T(8,128)S(1)}, u32[]{:S(2)}, u32[]{:S(2)}) %all-to-all-start) | async-done | bytes 1048608 | tf_op jit(solution)/shard_map/all_to_all | solution.py:95
  416.5 17.9 %while.30 = (s32[]{:T(128)}, f32[4,128,128]{2,1,0:T(8,128)S(1)}, f32[4,128,128]{2,1,0:T(8,128)S(1)}, f32[4,4,128,128]{3,2,0,1:T(8,128)}, f32[4,4,128,128]{2,3,0,...) while((s32[]{:T(128)}, f32[4,128,128]{2,1,0:T(8,128)S(1)}, ...), condition=%wide.region_3.4_spmd.clone, body=%wide.region_2.3_spmd.clone.sunk | while | flops 201523200 | bytes 4983400 | solution.py:82
  434.4 56.7 %while.28 = (s32[]{:T(128)}, f32[4,128,128]{2,1,0:T(8,128)S(1)}, f32[4,128,128]{2,1,0:T(8,128)S(1)}, f32[4,128,128]{2,1,0:T(8,128)S(1)}, s32[]{:T(128)}) while((s32[]{:T(128)}, f32[4,128,128]{2,1,0:T(8,128)S(1)}, f32[4,128,128]{2,1,0:T(8,128)S(1)}, f32[4,128,128]{2,1,0:T(8,128)S(1)}, s32[]{:T(128)}) %tuple.58), condition=%wide.region_5.6_spmd, body=%wide.region_4.5_spmd.sunk | while | flops 100728832 | bytes 2097253 | solution.py:107
  436.7 5.8 %collective-permute-done = f32[4,128,128]{2,1,0:T(8,128)S(1)} collective-permute-done((f32[4,128,128]{2,1,0:T(8,128)S(1)}, f32[4,128,128]{2,1,0:T(8,128)S(1)}, u32[]{:S(2)}, u32[]{:S(2)}) %collective-permute-start) | collective-permute-done | bytes 262176 | tf_op jit(solution)/shard_map/while/body/eval_jaxpr/ppermute | solution.py:12
  444.8 5.8 %collective-permute-done = f32[4,128,128]{2,1,0:T(8,128)S(1)} collective-permute-done((f32[4,128,128]{2,1,0:T(8,128)S(1)}, f32[4,128,128]{2,1,0:T(8,128)S(1)}, u32[]{:S(2)}, u32[]{:S(2)}) %collective-permute-start) | collective-permute-done | bytes 262176 | tf_op jit(solution)/shard_map/while/body/eval_jaxpr/ppermute | solution.py:12
  452.9 5.8 %collective-permute-done = f32[4,128,128]{2,1,0:T(8,128)S(1)} collective-permute-done((f32[4,128,128]{2,1,0:T(8,128)S(1)}, f32[4,128,128]{2,1,0:T(8,128)S(1)}, u32[]{:S(2)}, u32[]{:S(2)}) %collective-permute-start) | collective-permute-done | bytes 262176 | tf_op jit(solution)/shard_map/while/body/eval_jaxpr/ppermute | solution.py:12
  461.0 5.8 %collective-permute-done = f32[4,128,128]{2,1,0:T(8,128)S(1)} collective-permute-done((f32[4,128,128]{2,1,0:T(8,128)S(1)}, f32[4,128,128]{2,1,0:T(8,128)S(1)}, u32[]{:S(2)}, u32[]{:S(2)}) %collective-permute-start) | collective-permute-done | bytes 262176 | tf_op jit(solution)/shard_map/while/body/eval_jaxpr/ppermute | solution.py:12
  469.1 5.8 %collective-permute-done = f32[4,128,128]{2,1,0:T(8,128)S(1)} collective-permute-done((f32[4,128,128]{2,1,0:T(8,128)S(1)}, f32[4,128,128]{2,1,0:T(8,128)S(1)}, u32[]{:S(2)}, u32[]{:S(2)}) %collective-permute-start) | collective-permute-done | bytes 262176 | tf_op jit(solution)/shard_map/while/body/eval_jaxpr/ppermute | solution.py:12
  477.2 5.8 %collective-permute-done = f32[4,128,128]{2,1,0:T(8,128)S(1)} collective-permute-done((f32[4,128,128]{2,1,0:T(8,128)S(1)}, f32[4,128,128]{2,1,0:T(8,128)S(1)}, u32[]{:S(2)}, u32[]{:S(2)}) %collective-permute-start) | collective-permute-done | bytes 262176 | tf_op jit(solution)/shard_map/while/body/eval_jaxpr/ppermute | solution.py:12
  485.3 5.8 %collective-permute-done = f32[4,128,128]{2,1,0:T(8,128)S(1)} collective-permute-done((f32[4,128,128]{2,1,0:T(8,128)S(1)}, f32[4,128,128]{2,1,0:T(8,128)S(1)}, u32[]{:S(2)}, u32[]{:S(2)}) %collective-permute-start) | collective-permute-done | bytes 262176 | tf_op jit(solution)/shard_map/while/body/eval_jaxpr/ppermute | solution.py:12
  491.0 2.6 fusion.39
  494.8 4.5 all-to-all-start.2
  502.0 3.1 fusion.28
  506.5 3.3 fusion.36
  509.8 11.2 %all-to-all-done.2 = f32[4,4,128,128]{2,3,1,0:T(8,128)} async-done(((f32[4,4,128,128]{2,3,1,0:T(8,128)}), f32[4,4,128,128]{2,3,1,0:T(8,128)}, u32[]{:S(2)}, u32[]{:S(2)}) %all-to-all-start.2) | async-done | bytes 1048608 | tf_op jit(solution)/shard_map/all_to_all | solution.py:109
  521.0 3.8 fusion.67
  524.9 5.4 %multiply_reduce_fusion = (f32[16,128]{1,0:T(8,128)S(1)}, f32[16,128,128]{1,2,0:T(8,128)S(1)}) fusion(f32[16,128,128]{1,2,0:T(8,128)S(1)} %fusion.67, f32[16,128,256]{2,1,0:T(8,128)S(1)} %copy-done.2, f32[16,128,256]{2,1,0:T(8,128)} %copy-done.3, f32[16,128,256]{2,1,0:T(8,128)} %copy-done.5, pred[128,256]{1,0:T(8,128)(4,1)S(1)} %iota_compare_fusion.4), kind=kOutput, calls=%fused_computation.62 | convolution fusion | flops 807139328 | bytes 8429568 | tf_op jit(solution)/shard_map/hts,hse->hte/dot_general | solution.py:59
  (109 shorter events, 48.2 us)
Async XLA Ops:
  0.0 3.7 copy-start.8
  3.7 2.9 copy-start.12
  14.8 325.0 %copy-start.10 = (bf16[128,2,2048]{2,1,0:T(2,128)(2,1)S(1)}, bf16[128,2,2048]{2,1,0:T(2,128)(2,1)}, u32[]{:S(2)}) copy-start(bf16[128,2,2048]{2,1,0:T(2,128)(2,1)} %param.11) | copy-start | bytes 3145732
  339.9 1.6 copy-start.9
  343.5 6.2 %copy-start = (f32[16,128,256]{2,1,0:T(8,128)}, f32[16,128,256]{2,1,0:T(8,128)S(1)}, u32[]{:S(2)}) copy-start(f32[16,128,256]{2,1,0:T(8,128)S(1)} %fusion.13) | copy-start | bytes 6291460
  349.7 5.5 %copy-start.3 = (f32[16,128,256]{2,1,0:T(8,128)}, f32[16,128,256]{2,1,0:T(8,128)S(1)}, u32[]{:S(2)}) copy-start(f32[16,128,256]{2,1,0:T(8,128)S(1)} %fusion.16) | copy-start | bytes 6291460
  355.2 30.6 %all-to-all-start.1 = ((f32[1,4,4,128,128]{4,3,2,0,1:T(8,128)}), f32[1,4,4,128,128]{4,3,2,0,1:T(8,128)S(1)}, u32[]{:S(2)}, u32[]{:S(2)}) async-start(f32[1,4,4,128,128]{4,3,2,0,1:T(8,128)} %bitcast.127), calls=%async_computation.1 | async-start | bytes 2097152 | tf_op jit(solution)/shard_map/all_to_all | solution.py:96
  385.8 1.0 copy-start.7
  386.7 28.7 %all-to-all-start = ((f32[1,4,4,128,128]{4,3,2,0,1:T(8,128)}), f32[1,4,4,128,128]{4,3,2,0,1:T(8,128)S(1)}, u32[]{:S(2)}, u32[]{:S(2)}) async-start(f32[1,4,4,128,128]{4,3,2,0,1:T(8,128)} %bitcast.126), calls=%async_computation | async-start | bytes 2097152 | tf_op jit(solution)/shard_map/all_to_all | solution.py:95
  415.5 1.0 copy-start.6
  434.8 7.7 %collective-permute-start = (f32[4,128,128]{2,1,0:T(8,128)S(1)}, f32[4,128,128]{2,1,0:T(8,128)S(1)}, u32[]{:S(2)}, u32[]{:S(2)}) collective-permute-start(f32[4,128,128]{2,1,0:T(8,128)S(1)} %convolution_add_fusion.4), channel_id=1, source_target_pairs={{0,4},{4,8},{8,12},{12,16},{16,20},{20,24},{24,28},{1,5},{5,9},{9,... | collective-permute-start | bytes 786440 | tf_op jit(solution)/shard_map/while/body/eval_jaxpr/ppermute | solution.py:12
  442.9 7.7 %collective-permute-start = (f32[4,128,128]{2,1,0:T(8,128)S(1)}, f32[4,128,128]{2,1,0:T(8,128)S(1)}, u32[]{:S(2)}, u32[]{:S(2)}) collective-permute-start(f32[4,128,128]{2,1,0:T(8,128)S(1)} %convolution_add_fusion.4), channel_id=1, source_target_pairs={{0,4},{4,8},{8,12},{12,16},{16,20},{20,24},{24,28},{1,5},{5,9},{9,... | collective-permute-start | bytes 786440 | tf_op jit(solution)/shard_map/while/body/eval_jaxpr/ppermute | solution.py:12
  451.0 7.7 %collective-permute-start = (f32[4,128,128]{2,1,0:T(8,128)S(1)}, f32[4,128,128]{2,1,0:T(8,128)S(1)}, u32[]{:S(2)}, u32[]{:S(2)}) collective-permute-start(f32[4,128,128]{2,1,0:T(8,128)S(1)} %convolution_add_fusion.4), channel_id=1, source_target_pairs={{0,4},{4,8},{8,12},{12,16},{16,20},{20,24},{24,28},{1,5},{5,9},{9,... | collective-permute-start | bytes 786440 | tf_op jit(solution)/shard_map/while/body/eval_jaxpr/ppermute | solution.py:12
  459.1 7.7 %collective-permute-start = (f32[4,128,128]{2,1,0:T(8,128)S(1)}, f32[4,128,128]{2,1,0:T(8,128)S(1)}, u32[]{:S(2)}, u32[]{:S(2)}) collective-permute-start(f32[4,128,128]{2,1,0:T(8,128)S(1)} %convolution_add_fusion.4), channel_id=1, source_target_pairs={{0,4},{4,8},{8,12},{12,16},{16,20},{20,24},{24,28},{1,5},{5,9},{9,... | collective-permute-start | bytes 786440 | tf_op jit(solution)/shard_map/while/body/eval_jaxpr/ppermute | solution.py:12
  467.2 7.7 %collective-permute-start = (f32[4,128,128]{2,1,0:T(8,128)S(1)}, f32[4,128,128]{2,1,0:T(8,128)S(1)}, u32[]{:S(2)}, u32[]{:S(2)}) collective-permute-start(f32[4,128,128]{2,1,0:T(8,128)S(1)} %convolution_add_fusion.4), channel_id=1, source_target_pairs={{0,4},{4,8},{8,12},{12,16},{16,20},{20,24},{24,28},{1,5},{5,9},{9,... | collective-permute-start | bytes 786440 | tf_op jit(solution)/shard_map/while/body/eval_jaxpr/ppermute | solution.py:12
  475.3 7.7 %collective-permute-start = (f32[4,128,128]{2,1,0:T(8,128)S(1)}, f32[4,128,128]{2,1,0:T(8,128)S(1)}, u32[]{:S(2)}, u32[]{:S(2)}) collective-permute-start(f32[4,128,128]{2,1,0:T(8,128)S(1)} %convolution_add_fusion.4), channel_id=1, source_target_pairs={{0,4},{4,8},{8,12},{12,16},{16,20},{20,24},{24,28},{1,5},{5,9},{9,... | collective-permute-start | bytes 786440 | tf_op jit(solution)/shard_map/while/body/eval_jaxpr/ppermute | solution.py:12
  483.4 7.7 %collective-permute-start = (f32[4,128,128]{2,1,0:T(8,128)S(1)}, f32[4,128,128]{2,1,0:T(8,128)S(1)}, u32[]{:S(2)}, u32[]{:S(2)}) collective-permute-start(f32[4,128,128]{2,1,0:T(8,128)S(1)} %convolution_add_fusion.4), channel_id=1, source_target_pairs={{0,4},{4,8},{8,12},{12,16},{16,20},{20,24},{24,28},{1,5},{5,9},{9,... | collective-permute-start | bytes 786440 | tf_op jit(solution)/shard_map/while/body/eval_jaxpr/ppermute | solution.py:12
  493.6 5.7 %copy-start.11 = (bf16[128,2048]{1,0:T(8,128)(2,1)S(1)}, bf16[128,2048]{1,0:T(8,128)(2,1)}, u32[]{:S(2)}) copy-start(bf16[128,2048]{1,0:T(8,128)(2,1)} %param.9) | copy-start | bytes 1572868
  494.8 26.2 %all-to-all-start.2 = ((f32[4,4,128,128]{2,3,1,0:T(8,128)}), f32[4,4,128,128]{2,3,1,0:T(8,128)}, u32[]{:S(2)}, u32[]{:S(2)}) async-start(f32[4,4,128,128]{2,3,1,0:T(8,128)} %copy.105), calls=%async_computation.2 | async-start | bytes 2097152 | tf_op jit(solution)/shard_map/all_to_all | solution.py:109
  502.0 4.5 copy-start.1
  502.0 4.4 copy-start.4
  505.2 1.3 copy-start.5
  509.8 15.1 %copy-start.2 = (f32[16,128,256]{2,1,0:T(8,128)S(1)}, f32[16,128,256]{2,1,0:T(8,128)}, u32[]{:S(2)}) copy-start(f32[16,128,256]{2,1,0:T(8,128)} %copy-done) | copy-start | bytes 6291460
  524.9 5.5 %copy-start.13 = (f32[2048]{0:T(1024)S(1)}, f32[2048]{0:T(1024)}, u32[]{:S(2)}) copy-start(f32[2048]{0:T(1024)} %param.13) | copy-start | bytes 24580
where the time goes:
time: 538 us; the launch traced here: 532 us
  other arithmetic  326 us (61%)
  waiting for transfers between devices  95.6 us (18%)
  matrix products  58.2 us (11%)
  starting transfers between devices  26.3 us (5%)
  local copies, waits for them, and re-layouts  24.7 us (5%)
    another operation x3, other arithmetic, block_terms(): lax.linalg.triangular_solve(system, both, left_side=True, lower=True, uni...  316 us
    ppermute x7, waiting for transfers between devices, passed_along(): return lax.ppermute(value, axis, pairs)  40.3 us
    all_to_all x1, waiting for transfers between devices, local(): lax.all_to_all(trans_split, 'inner', split_axis=1, concat_axis=0, tiled=T...  25.2 us
    all_to_all x1, waiting for transfers between devices, local(): lax.all_to_all(offset_split, 'inner', split_axis=1, concat_axis=0, tiled=...  18.9 us
    dot_general x15, matrix products, matmul_heads(): return jnp.einsum('hde,hef->hdf', left, right, precision=HIGH)  13.8 us
    ppermute x7, starting transfers between devices, passed_along(): return lax.ppermute(value, axis, pairs)  13.4 us
    all_to_all x1, waiting for transfers between devices, local(): lax.all_to_all(entry, 'inner', split_axis=0, concat_axis=1, tiled=True)  11.2 us
  transfers between devices with their start and end apart: 10, of which 10 were waited for; matrix products, arithmetic and copies ran while one was open for 3% of the time, Pallas kernels for 0%

commit v1 on v0

v1 whole, which is shorter than its diff:
```python
import functools

import jax
import jax.numpy as jnp
from jax import lax
from jax.experimental import pallas as pl
from jax.experimental.pallas import tpu as pltpu
from jax.sharding import PartitionSpec as P

F32 = jnp.float32
BF16 = jnp.bfloat16
MESH = pl.DeviceIdType.MESH
GROUP = 4


def dot(a, b):
    return lax.dot_general(a, b, (((1,), (0,)), ((), ())), preferred_element_type=F32)


def dot_nt(a, b):
    return lax.dot_general(a, b, (((1,), (1,)), ((), ())), preferred_element_type=F32)


def dot_tn(a, b):
    return lax.dot_general(a, b, (((0,), (0,)), ((), ())), preferred_element_type=F32)


def split(x):
    hi = x.astype(BF16)
    return hi, (x - hi.astype(F32)).astype(BF16)


def dot3(a, b):
    ah, al = split(a)
    bh, bl = split(b)
    return dot(ah, bh) + (dot(ah, bl) + dot(al, bh))


def unit_lower_inverses(systems, masks):
    size = systems[0].shape[0]
    eye = masks[0]
    out = [eye - n * masks[1] for n in systems]
    levels = size.bit_length() - 2
    for level in range(levels):
        mask = masks[2 + level]
        mid = [dot(n * mask, t).astype(BF16) for n, t in zip(systems, out)]
        out = [t - dot(t, m).astype(BF16) for t, m in zip(out, mid)]
    return out


def level_masks(size):
    row = lax.broadcasted_iota(jnp.int32, (size, size), 0)
    col = lax.broadcasted_iota(jnp.int32, (size, size), 1)
    lower = row > col
    masks = [(row == col)]
    for level in range(size.bit_length() - 1):
        same = (row >> (level + 1)) == (col >> (level + 1))
        apart = (row >> level) != (col >> level)
        masks.append(lower & same & apart)
    return [m.astype(F32).astype(BF16) for m in masks]


def local_kernel(q_ref, k_ref, v_ref, b_ref, maps_ref, outs_ref, mask_ref):
    count = q_ref.shape[0]
    rows = k_ref.shape[0]
    size = maps_ref.shape[1]
    half = rows // 2
    n_heads = maps_ref.shape[0]

    @pl.when(pl.program_id(0) == 0)
    def _():
        for at, m in enumerate(level_masks(half)):
            mask_ref[at] = m

    masks = [mask_ref[at] for at in range(mask_ref.shape[0])]
    row_h = lax.broadcasted_iota(jnp.int32, (half, half), 0)
    col_h = lax.broadcasted_iota(jnp.int32, (half, half), 1)
    strict = row_h > col_h
    beta_all = 2.0 / (1.0 + jnp.exp(-b_ref[0]))
    heads = range(n_heads)
    cols = [slice(h * size, (h + 1) * size) for h in heads]
    k = [k_ref[:, c] for c in cols]
    n00, n10, n11, rhs = [], [], [], []
    for h in heads:
        kf = k[h].astype(F32)
        inv = 1.0 / (jnp.sum(kf * kf, axis=-1, keepdims=True) + 1e-06)
        beta = beta_all[:, h : h + 1]
        coef = beta * inv
        k0, k1 = k[h][:half], k[h][half:]
        n00.append(split(jnp.where(strict, coef[:half] * dot_nt(k0, k0), 0.0)))
        n11.append(split(jnp.where(strict, coef[half:] * dot_nt(k1, k1), 0.0)))
        n10.append(split(coef[half:] * dot_nt(k1, k0)))
        vf = v_ref[:, cols[h]].astype(F32) * (beta * jnp.sqrt(inv))
        rhs.append(jnp.concatenate([vf, kf * coef], axis=1))
    inverse = unit_lower_inverses([n[0] for n in n00] + [n[0] for n in n11], masks)

    def solve(t, n, r):
        zh = dot(t, r.astype(BF16)).astype(BF16)
        res = (r - zh.astype(F32)) - (dot(n[0], zh) + dot(n[1], zh))
        return zh, dot(t, res.astype(BF16)).astype(BF16)

    top = [solve(inverse[h], n00[h], rhs[h][:half]) for h in heads]
    low = []
    for h in heads:
        th, tl = top[h]
        r = rhs[h][half:] - (dot(n10[h][0], th) + (dot(n10[h][1], th) + dot(n10[h][0], tl)))
        low.append(solve(inverse[n_heads + h], n11[h], r))
    eye = (row_h == col_h).astype(F32)
    tok = lax.broadcasted_iota(jnp.int32, (count, rows), 0)
    virt = lax.broadcasted_iota(jnp.int32, (count, rows), 1)
    seen = virt <= 2 * tok + 1
    for h in heads:
        zh = jnp.concatenate([top[h][0], low[h][0]], axis=0)
        zl = jnp.concatenate([top[h][1], low[h][1]], axis=0)
        kz = dot_tn(k[h], zh) + dot_tn(k[h], zl)
        maps_ref[h, :, :size] = eye - kz[:, size:]
        maps_ref[h, :, size:] = kz[:, :size]
        q = q_ref[:, cols[h]]
        qf = q.astype(F32)
        rq = lax.rsqrt(jnp.sum(qf * qf, axis=-1, keepdims=True) + 1e-06)
        ph, plo = split(jnp.where(seen, dot_nt(q, k[h]), 0.0))
        pz = dot(ph, zh) + (dot(plo, zh) + dot(ph, zl))
        outs_ref[h, :, :size] = pz[:, :size] * rq
        outs_ref[h, :, size:] = (qf - pz[:, size:]) * rq


def local_terms(queries, keys, values, logits):
    count, width = queries.shape
    heads = logits.shape[1]
    size = width // heads
    rows = 2 * count
    group = GROUP
    steps = heads // group
    half = rows // 2
    k2 = keys.reshape(rows, width)
    v2 = values.reshape(rows, width)
    b2 = logits.transpose(1, 2, 0).reshape(steps, group, rows).transpose(0, 2, 1)
    span = group * size
    return pl.pallas_call(
        local_kernel,
        grid=(steps,),
        in_specs=[
            pl.BlockSpec((count, span), lambda s: (0, s)),
            pl.BlockSpec((rows, span), lambda s: (0, s)),
            pl.BlockSpec((rows, span), lambda s: (0, s)),
            pl.BlockSpec((1, rows, group), lambda s: (s, 0, 0)),
        ],
        out_specs=[
            pl.BlockSpec((group, size, 2 * size), lambda s: (s, 0, 0)),
            pl.BlockSpec((group, count, 2 * size), lambda s: (s, 0, 0)),
        ],
        out_shape=[
            jax.ShapeDtypeStruct((heads, size, 2 * size), F32),
            jax.ShapeDtypeStruct((heads, count, 2 * size), F32),
        ],
        scratch_shapes=[pltpu.VMEM((half.bit_length(), half, half), BF16)],
        compiler_params=pltpu.CompilerParams(vmem_limit_bytes=48 * 1024 * 1024),
    )(queries, k2, v2, b2)


def chain_kernel(
    n_in, n_out, maps_ref, outs_ref, gain_ref, mixed_ref,
    comp, pre, state, after, s_pre, r_pre, s_chain, s_relay, r_state,
):
    heads, size = maps_ref.shape[0], maps_ref.shape[1]
    at, grp = lax.axis_index("inner"), lax.axis_index("outer")
    first, last = at == 0, at == n_in - 1
    has_prev = last & (grp > 0)
    has_next = last & (grp < n_out - 1)

    barrier = pltpu.get_barrier_semaphore()

    def greet(cond, dev):
        @pl.when(cond)
        def _():
            pl.semaphore_signal(barrier, inc=1, device_id=dev, device_id_type=MESH)

    greet(at > 0, (grp, at - 1))
    greet(at < n_in - 1, (grp, at + 1))
    greet(has_prev, (grp - 1, at))
    greet(has_next, (grp + 1, at))
    peers = sum(c.astype(jnp.int32) for c in (at > 0, at < n_in - 1, has_prev, has_next))
    pl.semaphore_wait(barrier, peers)

    def send_pre(h):
        return pltpu.make_async_remote_copy(
            comp.at[h], pre.at[h], s_pre.at[h], r_pre.at[h],
            device_id=(grp, at + 1), device_id_type=MESH)

    def send_chain(h):
        return pltpu.make_async_remote_copy(
            after.at[h], state.at[h], s_chain.at[h], r_state.at[h],
            device_id=(grp + 1, at), device_id_type=MESH)

    def send_relay(h):
        return pltpu.make_async_remote_copy(
            state.at[h], state.at[h], s_relay.at[h], r_state.at[h],
            device_id=(grp, at - 1), device_id_type=MESH)

    def prefix(h, _):
        @pl.when(first)
        def _():
            comp[h] = maps_ref[h]

        @pl.when(jnp.logical_not(first))
        def _():
            send_pre(h).wait_recv()
            own = maps_ref[h]
            both = dot3(own[:, :size], pre[h])
            comp[h, :, :size] = both[:, :size]
            comp[h, :, size:] = both[:, size:] + own[:, size:]

        @pl.when(jnp.logical_not(last))
        def _():
            send_pre(h).start()

        return 0

    lax.fori_loop(0, heads, prefix, 0)

    def finish(h, _):
        @pl.when(jnp.logical_not(last) | (grp > 0))
        def _():
            send_chain(h).wait_recv()

        @pl.when(last & (grp == 0))
        def _():
            state[h] = jnp.zeros((size, size), F32)

        @pl.when(has_next)
        def _():
            after[h] = dot3(comp[h, :, :size], state[h]) + comp[h, :, size:]
            send_chain(h).start()

        @pl.when(at > 0)
        def _():
            send_relay(h).start()

        def emit(entry):
            outs = outs_ref[h, :, :size] + dot3(outs_ref[h, :, size:], entry)
            scale = lax.rsqrt(jnp.mean(outs * outs, axis=-1, keepdims=True) + 1e-06)
            where = pl.ds(pl.multiple_of(h * size, size), size)
            mixed_ref[:, where] = (outs * scale * gain_ref[:, where]).astype(BF16)

        @pl.when(first)
        def _():
            emit(state[h])

        @pl.when(jnp.logical_not(first))
        def _():
            emit(dot3(pre[h, :, :size], state[h]) + pre[h, :, size:])

        return 0

    lax.fori_loop(0, heads, finish, 0)

    def drain(h, _):
        @pl.when(jnp.logical_not(last))
        def _():
            send_pre(h).wait_send()

        @pl.when(has_next)
        def _():
            send_chain(h).wait_send()

        @pl.when(at > 0)
        def _():
            send_relay(h).wait_send()

        return 0

    lax.fori_loop(0, heads, drain, 0)


def chained(maps, outs, gain):
    heads, size, _ = maps.shape
    count = outs.shape[1]
    n_in, n_out = lax.axis_size("inner"), lax.axis_size("outer")
    vmem = pl.BlockSpec(memory_space=pltpu.VMEM)
    sems = pltpu.SemaphoreType.DMA((heads,))
    return pl.pallas_call(
        functools.partial(chain_kernel, n_in, n_out),
        out_shape=jax.ShapeDtypeStruct((count, heads * size), BF16),
        in_specs=[vmem] * 3,
        out_specs=vmem,
        scratch_shapes=[
            pltpu.VMEM((heads, size, 2 * size), F32),
            pltpu.VMEM((heads, size, 2 * size), F32),
            pltpu.VMEM((heads, size, size), F32),
            pltpu.VMEM((heads, size, size), F32),
            sems, sems, sems, sems, sems,
        ],
        compiler_params=pltpu.CompilerParams(
            collective_id=0, has_side_effects=True, vmem_limit_bytes=48 * 1024 * 1024
        ),
    )(maps, outs, gain.reshape(1, -1))


def local(queries, keys, values, beta_logit, gain):
    maps, outs = local_terms(queries, keys, values, beta_logit)
    return chained(maps, outs, gain)


def solution(mesh):
    return jax.shard_map(
        local,
        mesh=mesh,
        in_specs=(
            P(("outer", "inner"), None),
            P(("outer", "inner"), None, None),
            P(("outer", "inner"), None, None),
            P(None, None, ("outer", "inner")),
            P(),
        ),
        out_specs=P(("outer", "inner"), None),
        check_vma=False,
    )
```

time: 538 us -> 135 us (0.25); the launches traced: 532 us -> 135 us
  other arithmetic: 326 us -> 0 us
  Pallas kernels: 0 us -> 129 us
  waiting for transfers between devices: 95.6 us -> 0 us
  matrix products: 58.2 us -> 0 us
  starting transfers between devices: 26.3 us -> 0 us
  local copies, waits for them, and re-layouts: 24.7 us -> 5.57 us
    another operation x5 -> x0, other arithmetic: 316 us -> none  [the longest x3 316 us: block_terms(): lax.linalg.triangular_solve(system, both, left_side=True, lower=True, uni...]
    pallas_call x0 -> x2, Pallas kernels: none -> 129 us  [the longest x1 103 us: chained(): pl.pallas_call(functools.partial(chain_kernel, n_in, n_out), out_shape=ja...]
    all_to_all x3 -> x0, waiting for transfers between devices: 55.3 us -> none  [the longest x1 25.2 us: local(): lax.all_to_all(trans_split, 'inner', split_axis=1, concat_axis=0, tiled=T...]
    dot_general x23 -> x0, matrix products: 50.1 us -> none  [the longest x15 13.8 us: matmul_heads(): return jnp.einsum('hde,hef->hdf', left, right, precision=HIGH)]
    ppermute x7 -> x0, waiting for transfers between devices: 40.3 us -> none  [passed_along(): return lax.ppermute(value, axis, pairs)]
    ppermute x7 -> x0, starting transfers between devices: 13.4 us -> none  [passed_along(): return lax.ppermute(value, axis, pairs)]
    all_to_all x3 -> x0, starting transfers between devices: 12.9 us -> none  [the longest x1 4.87 us: local(): lax.all_to_all(offset_split, 'inner', split_axis=1, concat_axis=0, tiled=...]
    another operation x8 -> x0, local copies, waits for them, and re-layouts: 9.31 us -> none
  transfers between devices with their start and end apart: 10 -> 0, of which waited for: 10 -> 0; matrix products, arithmetic and copies ran while one was open for 3% -> 0% of each run, Pallas kernels for 0% -> 0%
where the time goes in v1:
time: 135 us
  Pallas kernels  129 us (96%)
  local copies, waits for them, and re-layouts  5.57 us (4%)
    pallas_call x1, Pallas kernels, chained(): pl.pallas_call(functools.partial(chain_kernel, n_in, n_out), out_shape=ja...  103 us
    pallas_call x1, Pallas kernels, local_terms(): pl.pallas_call(local_kernel, grid=(steps,), in_specs=[pl.BlockSpec((count...  25.5 us

profile of v1, /device:TPU:6, one launch (start us, length us, event | category | flops | bytes accessed | tf_op | source)
XLA Modules:
  0.0 134.5 jit_solution(7849891804933194243)
XLA Ops:
  0.0 0.0 copy-start.3
  0.0 0.9 copy.6
  0.9 0.3 reshape.14
  1.3 0.0 copy-done.3
  1.3 0.0 copy-start.1
  1.3 0.4 reshape.12.k_ref
  1.7 1.5 %reshape.13.v_ref = bf16[256,2048]{1,0:T(8,128)(2,1)S(1)} reshape(bf16[128,2,2048]{2,1,0:T(2,128)(2,1)} %param.7) | data formatting | bytes 2097152 | tf_op jit(solution)/shard_map/reshape | solution.py:136
  3.2 0.0 copy-done.1
  3.2 0.0 copy-start.2
  3.2 25.5 %shard_map.55 = (f32[16,128,256]{2,1,0:T(8,128)S(1)}, f32[16,128,256]{2,1,0:T(8,128)}) custom-call(bf16[128,2048]{1,0:T(8,128)(2,1)S(1)} %copy-done.1, bf16[256,2048]{1,0:T(8,128)(2,1)S(1)} %reshape.12.k_ref, bf16[256,2048]{1,0:T(8,128)(2,1)S(1)} %reshape.13.v_ref, f32[4,256,4]{2,1,0:T(8,128)S(1)} %bitcast.7), custom_call_target="tpu_custom_call" | custom-call | tf_op jit(solution)/shard_map/pallas_call | solution.py:139
  28.7 0.0 copy-done.2
  28.7 0.0 copy-start
  28.7 1.6 %copy-done = f32[16,128,256]{2,1,0:T(8,128)S(1)} copy-done((f32[16,128,256]{2,1,0:T(8,128)S(1)}, f32[16,128,256]{2,1,0:T(8,128)}, u32[]{:S(2)}) %copy-start) | copy-done | bytes 2097176
  30.3 103.4 %shard_map.56 = bf16[128,2048]{1,0:T(8,128)(2,1)S(1)} custom-call(f32[16,128,256]{2,1,0:T(8,128)S(1)} %get-tuple-element.7.maps_ref, f32[16,128,256]{2,1,0:T(8,128)S(1)} %copy-done, f32[1,2048]{1,0:T(1,128)S(1)} %bitcast.8), custom_call_target="tpu_custom_call" | custom-call | tf_op jit(solution)/shard_map/pallas_call | solution.py:281
  133.7 0.8 copy.11
  (1 shorter events, 0.0 us)
Async XLA Ops:
  0.0 1.3 copy-start.3
  1.3 1.9 %copy-start.1 = (bf16[128,2048]{1,0:T(8,128)(2,1)S(1)}, bf16[128,2048]{1,0:T(8,128)(2,1)}, u32[]{:S(2)}) copy-start(bf16[128,2048]{1,0:T(8,128)(2,1)} %q_ref.1) | copy-start | bytes 1572868
  3.2 25.5 %copy-start.2 = (f32[2048]{0:T(1024)S(1)}, f32[2048]{0:T(1024)}, u32[]{:S(2)}) copy-start(f32[2048]{0:T(1024)} %param.9) | copy-start | bytes 24580
  28.7 1.6 %copy-start = (f32[16,128,256]{2,1,0:T(8,128)S(1)}, f32[16,128,256]{2,1,0:T(8,128)}, u32[]{:S(2)}) copy-start(f32[16,128,256]{2,1,0:T(8,128)} %get-tuple-element.8.outs_ref) | copy-start | bytes 6291460

commit v2 on v0

v2 whole, which is shorter than its diff:
```python
import functools

import jax
import jax.numpy as jnp
from jax import lax
from jax.experimental import pallas as pl
from jax.experimental.pallas import tpu as pltpu
from jax.sharding import PartitionSpec as P

F32 = jnp.float32
BF16 = jnp.bfloat16
MESH = pl.DeviceIdType.MESH
GROUP = 4


def dot(a, b):
    return lax.dot_general(a, b, (((1,), (0,)), ((), ())), preferred_element_type=F32)


def dot_nt(a, b):
    return lax.dot_general(a, b, (((1,), (1,)), ((), ())), preferred_element_type=F32)


def dot_tn(a, b):
    return lax.dot_general(a, b, (((0,), (0,)), ((), ())), preferred_element_type=F32)


def split(x):
    hi = x.astype(BF16)
    return hi, (x - hi.astype(F32)).astype(BF16)


def dot3(a, b):
    ah, al = split(a)
    bh, bl = split(b)
    return dot(ah, bh) + (dot(ah, bl) + dot(al, bh))


def unit_lower_inverses(systems, masks):
    size = systems[0].shape[0]
    eye = masks[0]
    out = [eye - n * masks[1] for n in systems]
    levels = size.bit_length() - 2
    for level in range(levels):
        mask = masks[2 + level]
        mid = [dot(n * mask, t).astype(BF16) for n, t in zip(systems, out)]
        out = [t - dot(t, m).astype(BF16) for t, m in zip(out, mid)]
    return out


def level_masks(size):
    row = lax.broadcasted_iota(jnp.int32, (size, size), 0)
    col = lax.broadcasted_iota(jnp.int32, (size, size), 1)
    lower = row > col
    masks = [(row == col)]
    for level in range(size.bit_length() - 1):
        same = (row >> (level + 1)) == (col >> (level + 1))
        apart = (row >> level) != (col >> level)
        masks.append(lower & same & apart)
    return [m.astype(F32).astype(BF16) for m in masks]


def layer_kernel(
    n_in, n_out, q_ref, k_ref, v_ref, b_ref, gain_ref, mixed_ref,
    mask_ref, maps, zhi, zlo, outs, comp, pre, state, after, relay,
    s_pre, r_pre, s_chain, s_relay, r_state,
):
    heads, size = maps.shape[0], maps.shape[1]
    count, rows = q_ref.shape[0], k_ref.shape[0]
    half = rows // 2
    steps, group = b_ref.shape[0], b_ref.shape[2]
    span = group * size
    at, grp = lax.axis_index("inner"), lax.axis_index("outer")
    first, last = at == 0, at == n_in - 1
    inside = jnp.logical_not(first | last)
    has_prev = grp > 0
    has_next = grp < n_out - 1
    ends = first | last

    barrier = pltpu.get_barrier_semaphore()
    greetings = (
        (at > 0, (grp, at - 1)),
        (at < n_in - 1, (grp, at + 1)),
        (ends & has_prev, (grp - 1, at)),
        (ends & has_next, (grp + 1, at)),
    )
    for cond, dev in greetings:
        @pl.when(cond)
        def _():
            pl.semaphore_signal(barrier, inc=1, device_id=dev, device_id_type=MESH)

    for where, m in enumerate(level_masks(half)):
        mask_ref[where] = m
    pl.semaphore_wait(barrier, sum(c.astype(jnp.int32) for c, _ in greetings))

    def send_pre(h, fwd, src):
        return pltpu.make_async_remote_copy(
            src.at[h], pre.at[h], s_pre.at[h], r_pre.at[h],
            device_id=(grp, at + 1 if fwd else at - 1), device_id_type=MESH)

    def send_chain(h):
        return pltpu.make_async_remote_copy(
            after.at[h], state.at[h], s_chain.at[h], r_state.at[h],
            device_id=(grp + 1, at), device_id_type=MESH)

    def send_relay(h, fwd):
        src = state if fwd else relay
        return pltpu.make_async_remote_copy(
            src.at[h], state.at[h], s_relay.at[h], r_state.at[h],
            device_id=(grp, at - 1 if fwd else at + 1), device_id_type=MESH)

    row_h = lax.broadcasted_iota(jnp.int32, (half, half), 0)
    col_h = lax.broadcasted_iota(jnp.int32, (half, half), 1)
    span_of = [slice(h * size, (h + 1) * size) for h in range(group)]

    def lanes(step):
        return pl.ds(pl.multiple_of(step * span, span), span)

    def make_maps(step):
        masks = [mask_ref[m] for m in range(mask_ref.shape[0])]
        strict = row_h > col_h
        eye = (row_h == col_h).astype(F32)
        beta_all = 2.0 / (1.0 + jnp.exp(-b_ref[step]))
        k_all, v_all = k_ref[:, lanes(step)], v_ref[:, lanes(step)]
        k = [k_all[:, c] for c in span_of]
        n00, n10, n11, rhs = [], [], [], []
        for h in range(group):
            kf = k[h].astype(F32)
            inv = 1.0 / (jnp.sum(kf * kf, axis=-1, keepdims=True) + 1e-06)
            beta = beta_all[:, h : h + 1]
            coef = beta * inv
            k0, k1 = k[h][:half], k[h][half:]
            n00.append(split(jnp.where(strict, coef[:half] * dot_nt(k0, k0), 0.0)))
            n11.append(split(jnp.where(strict, coef[half:] * dot_nt(k1, k1), 0.0)))
            n10.append(split(coef[half:] * dot_nt(k1, k0)))
            vf = v_all[:, span_of[h]].astype(F32) * (beta * jnp.sqrt(inv))
            rhs.append(jnp.concatenate([vf, kf * coef], axis=1))
        inverse = unit_lower_inverses([n[0] for n in n00] + [n[0] for n in n11], masks)

        def solve(t, n, r):
            zh = dot(t, r.astype(BF16)).astype(BF16)
            res = (r - zh.astype(F32)) - (dot(n[0], zh) + dot(n[1], zh))
            return zh, dot(t, res.astype(BF16)).astype(BF16)

        top = [solve(inverse[h], n00[h], rhs[h][:half]) for h in range(group)]
        low = []
        for h in range(group):
            th, tl = top[h]
            r = rhs[h][half:] - (dot(n10[h][0], th) + (dot(n10[h][1], th) + dot(n10[h][0], tl)))
            low.append(solve(inverse[group + h], n11[h], r))
        for h in range(group):
            head = step * group + h
            zh = jnp.concatenate([top[h][0], low[h][0]], axis=0)
            zl = jnp.concatenate([top[h][1], low[h][1]], axis=0)
            kz = dot_tn(k[h], zh) + dot_tn(k[h], zl)
            maps[head, :, :size] = eye - kz[:, size:]
            maps[head, :, size:] = kz[:, :size]
            zhi[head] = zh
            zlo[head] = zl

    def make_outs(step):
        tok = lax.broadcasted_iota(jnp.int32, (count, rows), 0)
        virt = lax.broadcasted_iota(jnp.int32, (count, rows), 1)
        seen = virt <= 2 * tok + 1
        k_all, q_all = k_ref[:, lanes(step)], q_ref[:, lanes(step)]
        for h in range(group):
            head = step * group + h
            q = q_all[:, span_of[h]]
            qf = q.astype(F32)
            rq = lax.rsqrt(jnp.sum(qf * qf, axis=-1, keepdims=True) + 1e-06)
            ph, plo = split(jnp.where(seen, dot_nt(q, k_all[:, span_of[h]]), 0.0))
            zh = zhi[head]
            pz = dot(ph, zh) + (dot(plo, zh) + dot(ph, zlo[head]))
            outs[head, :, :size] = pz[:, :size] * rq
            outs[head, :, size:] = (qf - pz[:, size:]) * rq

    def prefix(h, fwd):
        start, end = (first, last) if fwd else (last, first)

        @pl.when(start)
        def _():
            send_pre(h, fwd, maps).start()

        @pl.when(jnp.logical_not(start))
        def _():
            send_pre(h, fwd, comp).wait_recv()
            own, got = maps[h], pre[h]
            late, early = (own, got) if fwd else (got, own)
            both = dot3(late[:, :size], early)
            comp[h, :, :size] = both[:, :size]
            comp[h, :, size:] = both[:, size:] + late[:, size:]

            @pl.when(jnp.logical_not(end))
            def _():
                send_pre(h, fwd, comp).start()

    def sweep(t, _):
        @pl.when(t < steps)
        def _():
            make_maps(t)

        @pl.when((t >= steps) & (t < 2 * steps))
        def _():
            make_outs(t - steps)

        fwd_step, bwd_step = t - 2 * at, t - 2 * (n_in - 1 - at)
        for pair in range(group // 2):
            @pl.when((fwd_step >= 0) & (fwd_step < steps))
            def _():
                prefix(fwd_step * group + 2 * pair, True)

            @pl.when((bwd_step >= 0) & (bwd_step < steps))
            def _():
                prefix(bwd_step * group + 2 * pair + 1, False)

        return 0

    lax.fori_loop(0, max(2 * steps, steps + 2 * (n_in - 1)), sweep, 0)

    def advance(src, h):
        return dot3(src[h, :, :size], state[h]) + src[h, :, size:]

    def link(j, _):
        for fwd in (True, False):
            h = 2 * j + (0 if fwd else 1)
            end = last if fwd else first

            @pl.when(end & has_prev)
            def _():
                send_chain(h).wait_recv()

            @pl.when(end & jnp.logical_not(has_prev))
            def _():
                state[h] = jnp.zeros((size, size), F32)

            @pl.when(end & has_next)
            def _():
                after[h] = advance(comp, h)
                send_chain(h).start()

            @pl.when(end)
            def _():
                if not fwd:
                    relay[h] = advance(maps, h)
                send_relay(h, fwd).start()

        return 0

    @pl.when(ends)
    def _():
        lax.fori_loop(0, heads // 2, link, 0)

    def finish(j, _):
        for fwd in (True, False):
            h = 2 * j + (0 if fwd else 1)
            start, end = (first, last) if fwd else (last, first)

            @pl.when(jnp.logical_not(end))
            def _():
                send_relay(h, fwd).wait_recv()

            @pl.when(inside)
            def _():
                if not fwd:
                    relay[h] = advance(maps, h)
                send_relay(h, fwd).start()

            def emit(entry):
                full = outs[h, :, :size] + dot3(outs[h, :, size:], entry)
                scale = lax.rsqrt(jnp.mean(full * full, axis=-1, keepdims=True) + 1e-06)
                where = pl.ds(pl.multiple_of(h * size, size), size)
                mixed_ref[:, where] = (full * scale * gain_ref[:, where]).astype(BF16)

            if fwd:
                @pl.when(start)
                def _():
                    emit(state[h])

                @pl.when(jnp.logical_not(start))
                def _():
                    emit(advance(pre, h))
            else:
                emit(state[h])

        return 0

    lax.fori_loop(0, heads // 2, finish, 0)

    def drain(j, _):
        for fwd in (True, False):
            h = 2 * j + (0 if fwd else 1)
            start, end = (first, last) if fwd else (last, first)

            @pl.when(jnp.logical_not(end))
            def _():
                send_pre(h, fwd, comp).wait_send()

            @pl.when(end & has_next)
            def _():
                send_chain(h).wait_send()

            @pl.when(jnp.logical_not(start))
            def _():
                send_relay(h, fwd).wait_send()

        return 0

    lax.fori_loop(0, heads // 2, drain, 0)


def local(queries, keys, values, beta_logit, gain):
    count, width = queries.shape
    heads = beta_logit.shape[1]
    size = width // heads
    rows = 2 * count
    steps = heads // GROUP
    half = rows // 2
    n_in, n_out = lax.axis_size("inner"), lax.axis_size("outer")
    k2 = keys.reshape(rows, width)
    v2 = values.reshape(rows, width)
    b2 = beta_logit.transpose(1, 2, 0).reshape(steps, GROUP, rows).transpose(0, 2, 1)
    vmem = pl.BlockSpec(memory_space=pltpu.VMEM)
    sems = pltpu.SemaphoreType.DMA((heads,))
    wide = pltpu.VMEM((heads, size, 2 * size), F32)
    square = pltpu.VMEM((heads, size, size), F32)
    solved = pltpu.VMEM((heads, rows, 2 * size), BF16)
    return pl.pallas_call(
        functools.partial(layer_kernel, n_in, n_out),
        out_shape=jax.ShapeDtypeStruct((count, width), BF16),
        in_specs=[vmem] * 5,
        out_specs=vmem,
        scratch_shapes=[
            pltpu.VMEM((half.bit_length(), half, half), BF16),
            wide, solved, solved,
            pltpu.VMEM((heads, count, 2 * size), F32),
            wide, wide, square, square, square,
            sems, sems, sems, sems, sems,
        ],
        compiler_params=pltpu.CompilerParams(
            collective_id=0, has_side_effects=True, vmem_limit_bytes=48 * 1024 * 1024
        ),
    )(queries, k2, v2, b2, gain.reshape(1, -1))


def solution(mesh):
    return jax.shard_map(
        local,
        mesh=mesh,
        in_specs=(
            P(("outer", "inner"), None),
            P(("outer", "inner"), None, None),
            P(("outer", "inner"), None, None),
            P(None, None, ("outer", "inner")),
            P(),
        ),
        out_specs=P(("outer", "inner"), None),
        check_vma=False,
    )
```

time: 538 us -> 137 us (0.25)
  other arithmetic: 326 us -> 0 us
  Pallas kernels: 0 us -> 130 us
  waiting for transfers between devices: 95.6 us -> 0 us
  matrix products: 58.2 us -> 0 us
  starting transfers between devices: 26.3 us -> 0 us
  local copies, waits for them, and re-layouts: 24.7 us -> 4.03 us
    another operation x5 -> x0, other arithmetic: 316 us -> none  [the longest x3 316 us: block_terms(): lax.linalg.triangular_solve(system, both, left_side=True, lower=True, uni...]
    pallas_call x0 -> x1, Pallas kernels: none -> 130 us  [local(): pl.pallas_call(functools.partial(layer_kernel, n_in, n_out), out_shape=ja...]
    all_to_all x3 -> x0, waiting for transfers between devices: 55.3 us -> none  [the longest x1 25.2 us: local(): lax.all_to_all(trans_split, 'inner', split_axis=1, concat_axis=0, tiled=T...]
    dot_general x23 -> x0, matrix products: 50.1 us -> none  [the longest x15 13.8 us: matmul_heads(): return jnp.einsum('hde,hef->hdf', left, right, precision=HIGH)]
    ppermute x7 -> x0, waiting for transfers between devices: 40.3 us -> none  [passed_along(): return lax.ppermute(value, axis, pairs)]
    ppermute x7 -> x0, starting transfers between devices: 13.4 us -> none  [passed_along(): return lax.ppermute(value, axis, pairs)]
    all_to_all x3 -> x0, starting transfers between devices: 12.9 us -> none  [the longest x1 4.87 us: local(): lax.all_to_all(offset_split, 'inner', split_axis=1, concat_axis=0, tiled=...]
    another operation x8 -> x0, local copies, waits for them, and re-layouts: 9.31 us -> none
  transfers between devices with their start and end apart: 10 -> 0, of which waited for: 10 -> 0; matrix products, arithmetic and copies ran while one was open for 3% -> 0% of each run, Pallas kernels for 0% -> 0%
where the time goes in v2:
time: 137 us; the launch traced here: 135 us
  Pallas kernels  130 us (95%)
  local copies, waits for them, and re-layouts  4.03 us (3%)
    pallas_call x1, Pallas kernels, local(): pl.pallas_call(functools.partial(layer_kernel, n_in, n_out), out_shape=ja...  130 us

profile of v2, /device:TPU:6, one launch (start us, length us, event | category | flops | bytes accessed | tf_op | source)
XLA Modules:
  0.0 134.6 jit_solution(14684350577553893674)
XLA Ops:
  0.0 0.0 copy-start.2
  0.0 0.9 copy.6
  0.9 0.3 reshape.14
  1.3 0.0 copy-done.2
  1.3 0.4 reshape.12.k_ref
  1.7 0.0 copy-start
  1.7 0.0 copy-start.1
  1.8 1.5 %reshape.13.v_ref = bf16[256,2048]{1,0:T(8,128)(2,1)S(1)} reshape(bf16[128,2,2048]{2,1,0:T(2,128)(2,1)} %param.7) | data formatting | bytes 2097152 | tf_op jit(solution)/shard_map/reshape | solution.py:320
  3.3 0.0 copy-done
  3.3 0.0 copy-done.1
  3.3 130.5 %shard_map.55 = bf16[128,2048]{1,0:T(8,128)(2,1)S(1)} custom-call(bf16[128,2048]{1,0:T(8,128)(2,1)S(1)} %copy-done, bf16[256,2048]{1,0:T(8,128)(2,1)S(1)} %reshape.12.k_ref, bf16[256,2048]{1,0:T(8,128)(2,1)S(1)} %reshape.13.v_ref, f32[4,256,4]{2,1,0:T(8,128)S(1)} %bitcast.7, f32[1,2048]{1,0:T(1,128)S(1)} %bitcast.8), custom_call_target="tpu_custom_call" | custom-call | tf_op jit(solution)/shard_map/pallas_call | solution.py:327
  133.8 0.8 copy.11
  (1 shorter events, 0.0 us)
Async XLA Ops:
  0.0 1.3 copy-start.2
  1.7 1.6 %copy-start = (bf16[128,2048]{1,0:T(8,128)(2,1)S(1)}, bf16[128,2048]{1,0:T(8,128)(2,1)}, u32[]{:S(2)}) copy-start(bf16[128,2048]{1,0:T(8,128)(2,1)} %q_ref.1) | copy-start | bytes 1572868
  1.7 1.6 %copy-start.1 = (f32[2048]{0:T(1024)S(1)}, f32[2048]{0:T(1024)}, u32[]{:S(2)}) copy-start(f32[2048]{0:T(1024)} %param.9) | copy-start | bytes 24580

commit v3 on v2

--- a/solution.py
+++ b/solution.py
@@ -10,7 +10,7 @@
 F32 = jnp.float32
 BF16 = jnp.bfloat16
 MESH = pl.DeviceIdType.MESH
-GROUP = 4
+GROUP = 2
 
 
 def dot(a, b):
@@ -72,7 +72,6 @@
     span = group * size
     at, grp = lax.axis_index("inner"), lax.axis_index("outer")
     first, last = at == 0, at == n_in - 1
-    inside = jnp.logical_not(first | last)
     has_prev = grp > 0
     has_next = grp < n_out - 1
     ends = first | last
@@ -155,8 +154,8 @@
             kz = dot_tn(k[h], zh) + dot_tn(k[h], zl)
             maps[head, :, :size] = eye - kz[:, size:]
             maps[head, :, size:] = kz[:, :size]
-            zhi[head] = zh
-            zlo[head] = zl
+            zhi[h] = zh
+            zlo[h] = zl
 
     def make_outs(step):
         tok = lax.broadcasted_iota(jnp.int32, (count, rows), 0)
@@ -169,8 +168,8 @@
             qf = q.astype(F32)
             rq = lax.rsqrt(jnp.sum(qf * qf, axis=-1, keepdims=True) + 1e-06)
             ph, plo = split(jnp.where(seen, dot_nt(q, k_all[:, span_of[h]]), 0.0))
-            zh = zhi[head]
-            pz = dot(ph, zh) + (dot(plo, zh) + dot(ph, zlo[head]))
+            zh = zhi[h]
+            pz = dot(ph, zh) + (dot(plo, zh) + dot(ph, zlo[h]))
             outs[head, :, :size] = pz[:, :size] * rq
             outs[head, :, size:] = (qf - pz[:, size:]) * rq
 
@@ -194,97 +193,87 @@
             def _():
                 send_pre(h, fwd, comp).start()
 
+    def advance(src, h):
+        return dot3(src[h, :, :size], state[h]) + src[h, :, size:]
+
+    def enter(h, fwd):
+        end = last if fwd else first
+
+        @pl.when(end & has_prev)
+        def _():
+            send_chain(h).wait_recv()
+
+        @pl.when(end & jnp.logical_not(has_prev))
+        def _():
+            state[h] = jnp.zeros((size, size), F32)
+
+        @pl.when(end & has_next)
+        def _():
+            after[h] = advance(comp, h)
+            send_chain(h).start()
+
+        @pl.when(jnp.logical_not(end))
+        def _():
+            send_relay(h, fwd).wait_recv()
+
+        @pl.when(jnp.logical_not(first if fwd else last))
+        def _():
+            if not fwd:
+                relay[h] = advance(maps, h)
+            send_relay(h, fwd).start()
+
+    def emit(h, fwd):
+        def write(entry):
+            full = outs[h, :, :size] + dot3(outs[h, :, size:], entry)
+            scale = lax.rsqrt(jnp.mean(full * full, axis=-1, keepdims=True) + 1e-06)
+            where = pl.ds(pl.multiple_of(h * size, size), size)
+            mixed_ref[:, where] = (full * scale * gain_ref[:, where]).astype(BF16)
+
+        if fwd:
+            @pl.when(first)
+            def _():
+                write(state[h])
+
+            @pl.when(jnp.logical_not(first))
+            def _():
+                write(advance(pre, h))
+        else:
+            write(state[h])
+
+    back = n_in - 1 - at
+    shift = n_in + grp // 2
+    pairs = (
+        (0, True, jnp.where(first, 0, at + 1), shift + back),
+        (1, False, jnp.where(last, 0, back + 1), shift + at),
+    )
+
     def sweep(t, _):
         @pl.when(t < steps)
         def _():
             make_maps(t)
 
-        @pl.when((t >= steps) & (t < 2 * steps))
-        def _():
-            make_outs(t - steps)
-
-        fwd_step, bwd_step = t - 2 * at, t - 2 * (n_in - 1 - at)
-        for pair in range(group // 2):
-            @pl.when((fwd_step >= 0) & (fwd_step < steps))
-            def _():
-                prefix(fwd_step * group + 2 * pair, True)
-
-            @pl.when((bwd_step >= 0) & (bwd_step < steps))
-            def _():
-                prefix(bwd_step * group + 2 * pair + 1, False)
+        for off, fwd, skew, _ in pairs:
+            @pl.when((t >= skew) & (t < steps + skew))
+            def _():
+                prefix((t - skew) * 2 + off, fwd)
+
+        for off, fwd, _, skew in pairs:
+            @pl.when((t >= skew) & (t < steps + skew))
+            def _():
+                enter((t - skew) * 2 + off, fwd)
+
+        @pl.when(t < steps)
+        def _():
+            make_outs(t)
+
+        for off, fwd, _, skew in pairs:
+            @pl.when((t >= skew) & (t < steps + skew))
+            def _():
+                emit((t - skew) * 2 + off, fwd)
 
         return 0
 
-    lax.fori_loop(0, max(2 * steps, steps + 2 * (n_in - 1)), sweep, 0)
-
-    def advance(src, h):
-        return dot3(src[h, :, :size], state[h]) + src[h, :, size:]
-
-    def link(j, _):
-        for fwd in (True, False):
-            h = 2 * j + (0 if fwd else 1)
-            end = last if fwd else first
-
-            @pl.when(end & has_prev)
-            def _():
-                send_chain(h).wait_recv()
-
-            @pl.when(end & jnp.logical_not(has_prev))
-            def _():
-                state[h] = jnp.zeros((size, size), F32)
-
-            @pl.when(end & has_next)
-            def _():
-                after[h] = advance(comp, h)
-                send_chain(h).start()
-
-            @pl.when(end)
-            def _():
-                if not fwd:
-                    relay[h] = advance(maps, h)
-                send_relay(h, fwd).start()
-
-        return 0
-
-    @pl.when(ends)
-    def _():
-        lax.fori_loop(0, heads // 2, link, 0)
-
-    def finish(j, _):
-        for fwd in (True, False):
-            h = 2 * j + (0 if fwd else 1)
-            start, end = (first, last) if fwd else (last, first)
-
-            @pl.when(jnp.logical_not(end))
-            def _():
-                send_relay(h, fwd).wait_recv()
-
-            @pl.when(inside)
-            def _():
-                if not fwd:
-                    relay[h] = advance(maps, h)
-                send_relay(h, fwd).start()
-
-            def emit(entry):
-                full = outs[h, :, :size] + dot3(outs[h, :, size:], entry)
-                scale = lax.rsqrt(jnp.mean(full * full, axis=-1, keepdims=True) + 1e-06)
-                where = pl.ds(pl.multiple_of(h * size, size), size)
-                mixed_ref[:, where] = (full * scale * gain_ref[:, where]).astype(BF16)
-
-            if fwd:
-                @pl.when(start)
-                def _():
-                    emit(state[h])
-
-                @pl.when(jnp.logical_not(start))
-                def _():
-                    emit(advance(pre, h))
-            else:
-                emit(state[h])
-
-        return 0
-
-    lax.fori_loop(0, heads // 2, finish, 0)
+    lax.fori_loop(0, steps + 2 * n_in + n_out // 2, sweep, 0)
 
     def drain(j, _):
         for fwd in (True, False):
@@ -323,7 +312,7 @@
     sems = pltpu.SemaphoreType.DMA((heads,))
     wide = pltpu.VMEM((heads, size, 2 * size), F32)
     square = pltpu.VMEM((heads, size, size), F32)
-    solved = pltpu.VMEM((heads, rows, 2 * size), BF16)
+    solved = pltpu.VMEM((GROUP, rows, 2 * size), BF16)
     return pl.pallas_call(
         functools.partial(layer_kernel, n_in, n_out),
         out_shape=jax.ShapeDtypeStruct((count, width), BF16),

time: 137 us -> 91 us (0.66); the launches traced: 135 us -> 90.7 us
  Pallas kernels: 130 us -> 84.8 us
  local copies, waits for them, and re-layouts: 4.03 us -> 5.75 us
    pallas_call x1, Pallas kernels: 130 us -> 84.8 us  [local(): pl.pallas_call(functools.partial(layer_kernel, n_in, n_out), out_shape=ja...]
    unnamed x7 -> x9, local copies, waits for them, and re-layouts: 0.81 us -> 2.43 us
where the time goes in v3:
time: 91 us; the launch traced here: 90.7 us
  Pallas kernels  84.8 us (93%)
  local copies, waits for them, and re-layouts  5.75 us (6%)
    pallas_call x1, Pallas kernels, local(): pl.pallas_call(functools.partial(layer_kernel, n_in, n_out), out_shape=ja...  84.8 us
    unnamed x9, local copies, waits for them, and re-layouts  2.43 us

profile of v3, /device:TPU:6, one launch (start us, length us, event | category | flops | bytes accessed | tf_op | source)
XLA Modules:
  0.0 90.7 jit_solution(9837139512293057456)
XLA Ops:
  0.0 0.0 copy-start.2
  0.0 1.6 %reshape.12.k_ref = bf16[256,2048]{1,0:T(8,128)(2,1)S(1)} reshape(bf16[128,2,2048]{2,1,0:T(2,128)(2,1)} %param.6) | data formatting | bytes 2097152 | tf_op jit(solution)/shard_map/reshape | solution.py:308
  1.6 0.0 copy-done.2
  1.6 0.0 copy-start.3
  1.6 0.4 reshape.13.v_ref
  2.0 0.3 copy-done.3
  2.3 0.4 copy.6
  2.7 0.6 reshape.14
  3.3 0.0 copy-start.1
  3.3 0.4 copy.7
  3.7 0.3 copy-done.1
  4.0 0.0 copy-start
  4.0 1.0 %copy-done = bf16[128,2048]{1,0:T(8,128)(2,1)S(1)} copy-done((bf16[128,2048]{1,0:T(8,128)(2,1)S(1)}, bf16[128,2048]{1,0:T(8,128)(2,1)}, u32[]{:S(2)}) %copy-start) | copy-done | bytes 524312
  5.0 84.8 %shard_map.55 = bf16[128,2048]{1,0:T(8,128)(2,1)S(1)} custom-call(bf16[128,2048]{1,0:T(8,128)(2,1)S(1)} %copy-done, bf16[256,2048]{1,0:T(8,128)(2,1)S(1)} %reshape.12.k_ref, bf16[256,2048]{1,0:T(8,128)(2,1)S(1)} %reshape.13.v_ref, f32[8,256,2]{2,1,0:T(8,128)S(1)} %bitcast.3, f32[1,2048]{1,0:T(1,128)S(1)} %bitcast.4), custom_call_target="tpu_custom_call" | custom-call | tf_op jit(solution)/shard_map/pallas_call | solution.py:316
  89.9 0.8 copy.9
Async XLA Ops:
  0.0 1.6 %copy-start.2 = (bf16[128,2,2048]{2,1,0:T(2,128)(2,1)S(1)}, bf16[128,2,2048]{2,1,0:T(2,128)(2,1)}, u32[]{:S(2)}) copy-start(bf16[128,2,2048]{2,1,0:T(2,128)(2,1)} %param.7) | copy-start | bytes 3145732
  1.6 0.7 copy-start.3
  3.3 0.7 copy-start.1
  4.0 1.0 %copy-start = (bf16[128,2048]{1,0:T(8,128)(2,1)S(1)}, bf16[128,2048]{1,0:T(8,128)(2,1)}, u32[]{:S(2)}) copy-start(bf16[128,2048]{1,0:T(8,128)(2,1)} %q_ref.1) | copy-start | bytes 1572868

commit v4 on v3

--- a/solution.py
+++ b/solution.py
@@ -10,7 +10,7 @@
 F32 = jnp.float32
 BF16 = jnp.bfloat16
 MESH = pl.DeviceIdType.MESH
-GROUP = 2
+GROUP = 4
 
 
 def dot(a, b):
@@ -62,13 +62,14 @@
 
 def layer_kernel(
     n_in, n_out, q_ref, k_ref, v_ref, b_ref, gain_ref, mixed_ref,
-    mask_ref, maps, zhi, zlo, outs, comp, pre, state, after, relay,
+    mask_ref, beta_ref, maps, zhi, zlo, outs, comp, pre, state, after, relay,
     s_pre, r_pre, s_chain, s_relay, r_state,
 ):
     heads, size = maps.shape[0], maps.shape[1]
     count, rows = q_ref.shape[0], k_ref.shape[0]
     half = rows // 2
-    steps, group = b_ref.shape[0], b_ref.shape[2]
+    steps, group = beta_ref.shape[0], beta_ref.shape[2]
+    n_pairs, pairs_at_once = heads // 2, group // 2
     span = group * size
     at, grp = lax.axis_index("inner"), lax.axis_index("outer")
     first, last = at == 0, at == n_in - 1
@@ -90,6 +91,18 @@
 
     for where, m in enumerate(level_masks(half)):
         mask_ref[where] = m
+    spot = lax.broadcasted_iota(jnp.int32, (rows, count), 0)
+    token = lax.broadcasted_iota(jnp.int32, (rows, count), 1)
+    spread = jnp.zeros((rows, heads), F32)
+    for j in range(2):
+        pick = (spot == 2 * token + j).astype(F32).astype(BF16)
+        strength = 2.0 / (1.0 + jnp.exp(-b_ref[j]))
+        for _ in range(3):
+            part = strength.astype(BF16)
+            strength = strength - part.astype(F32)
+            spread = spread + dot_nt(pick, part)
+    for step in range(steps):
+        beta_ref[step] = spread[:, step * group : (step + 1) * group]
     pl.semaphore_wait(barrier, sum(c.astype(jnp.int32) for c, _ in greetings))
 
     def send_pre(h, fwd, src):
@@ -119,7 +132,7 @@
         masks = [mask_ref[m] for m in range(mask_ref.shape[0])]
         strict = row_h > col_h
         eye = (row_h == col_h).astype(F32)
-        beta_all = 2.0 / (1.0 + jnp.exp(-b_ref[step]))
+        beta_all = beta_ref[step]
         k_all, v_all = k_ref[:, lanes(step)], v_ref[:, lanes(step)]
         k = [k_all[:, c] for c in span_of]
         n00, n10, n11, rhs = [], [], [], []
@@ -222,23 +235,15 @@
                 relay[h] = advance(maps, h)
             send_relay(h, fwd).start()
 
-    def emit(h, fwd):
-        def write(entry):
+    def emit(j):
+        def write(h, entry):
             full = outs[h, :, :size] + dot3(outs[h, :, size:], entry)
             scale = lax.rsqrt(jnp.mean(full * full, axis=-1, keepdims=True) + 1e-06)
             where = pl.ds(pl.multiple_of(h * size, size), size)
             mixed_ref[:, where] = (full * scale * gain_ref[:, where]).astype(BF16)
 
-        if fwd:
-            @pl.when(first)
-            def _():
-                write(state[h])
-
-            @pl.when(jnp.logical_not(first))
-            def _():
-                write(advance(pre, h))
-        else:
-            write(state[h])
+        write(2 * j + 1, state[2 * j + 1])
+        write(2 * j, advance(pre, 2 * j))
 
     back = n_in - 1 - at
     shift = n_in + grp // 2
@@ -246,34 +251,43 @@
         (0, True, jnp.where(first, 0, at + 1), shift + back),
         (1, False, jnp.where(last, 0, back + 1), shift + at),
     )
+    leave = shift + n_in - 1
+
+    @pl.when(first)
+    def _():
+        unit = jnp.concatenate(
+            [(row_h == col_h).astype(F32), jnp.zeros((size, size), F32)], axis=1)
+        for j in range(n_pairs):
+            pre[2 * j] = unit
 
     def sweep(t, _):
-        @pl.when(t < steps)
-        def _():
-            make_maps(t)
+        part = t % pairs_at_once
+
+        @pl.when((t < n_pairs) & (part == 0))
+        def _():
+            make_maps(t // pairs_at_once)
 
         for off, fwd, skew, _ in pairs:
-            @pl.when((t >= skew) & (t < steps + skew))
+            @pl.when((t >= skew) & (t < n_pairs + skew))
             def _():
                 prefix((t - skew) * 2 + off, fwd)
 
         for off, fwd, _, skew in pairs:
-            @pl.when((t >= skew) & (t < steps + skew))
+            @pl.when((t >= skew) & (t < n_pairs + skew))
             def _():
                 enter((t - skew) * 2 + off, fwd)
 
-        @pl.when(t < steps)
-        def _():
-            make_outs(t)
-
-        for off, fwd, _, skew in pairs:
-            @pl.when((t >= skew) & (t < steps + skew))
-            def _():
-                emit((t - skew) * 2 + off, fwd)
+        @pl.when((t < n_pairs) & (part == pairs_at_once - 1))
+        def _():
+            make_outs(t // pairs_at_once)
+
+        @pl.when((t >= leave) & (t < n_pairs + leave))
+        def _():
+            emit(t - leave)
 
         return 0
 
-    lax.fori_loop(0, steps + 2 * n_in + n_out // 2, sweep, 0)
+    lax.fori_loop(0, n_pairs + 2 * n_in + n_out // 2, sweep, 0)
 
     def drain(j, _):
         for fwd in (True, False):
@@ -307,7 +321,6 @@
     n_in, n_out = lax.axis_size("inner"), lax.axis_size("outer")
     k2 = keys.reshape(rows, width)
     v2 = values.reshape(rows, width)
-    b2 = beta_logit.transpose(1, 2, 0).reshape(steps, GROUP, rows).transpose(0, 2, 1)
     vmem = pl.BlockSpec(memory_space=pltpu.VMEM)
     sems = pltpu.SemaphoreType.DMA((heads,))
     wide = pltpu.VMEM((heads, size, 2 * size), F32)
@@ -320,6 +333,7 @@
         out_specs=vmem,
         scratch_shapes=[
             pltpu.VMEM((half.bit_length(), half, half), BF16),
+            pltpu.VMEM((steps, rows, GROUP), F32),
             wide, solved, solved,
             pltpu.VMEM((heads, count, 2 * size), F32),
             wide, wide, square, square, square,
@@ -328,7 +342,7 @@
         compiler_params=pltpu.CompilerParams(
             collective_id=0, has_side_effects=True, vmem_limit_bytes=48 * 1024 * 1024
         ),
-    )(queries, k2, v2, b2, gain.reshape(1, -1))
+    )(queries, k2, v2, beta_logit, gain.reshape(1, -1))
 
 
 def solution(mesh):

time: 91 us -> 90.4 us (level)
  local copies, waits for them, and re-layouts: 5.75 us -> 3.8 us
  Pallas kernels: 84.8 us -> 86.2 us
    unnamed x9 -> x7, local copies, waits for them, and re-layouts: 2.43 us -> 0.81 us
    pallas_call x1, Pallas kernels: 84.8 us -> 86.2 us  [local(): pl.pallas_call(functools.partial(layer_kernel, n_in, n_out), out_shape=ja...]
    reshape x1, local copies, waits for them, and re-layouts: 0.44 us -> 1.52 us  [local(): v2 = values.reshape(rows, width)]
    reshape x2 -> x0, local copies, waits for them, and re-layouts: 0.97 us -> none  [local(): beta_logit.transpose(1, 2, 0).reshape(steps, GROUP, rows).transpose(0, 2, 1)]
where the time goes in v4:
time: 90.4 us; the launch traced here: 90 us
  Pallas kernels  86.2 us (95%)
  local copies, waits for them, and re-layouts  3.8 us (4%)
    pallas_call x1, Pallas kernels, local(): pl.pallas_call(functools.partial(layer_kernel, n_in, n_out), out_shape=ja...  86.2 us

profile of v4, /device:TPU:6, one launch (start us, length us, event | category | flops | bytes accessed | tf_op | source)
XLA Modules:
  0.0 90.0 jit_solution(1458129998459038178)
XLA Ops:
  0.0 1.5 %reshape.9.k_ref = bf16[256,2048]{1,0:T(8,128)(2,1)S(1)} reshape(bf16[128,2,2048]{2,1,0:T(2,128)(2,1)} %param.6) | data formatting | bytes 2097152 | tf_op jit(solution)/shard_map/reshape | solution.py:322
  1.5 0.0 copy-start
  1.5 0.0 copy-start.1
  1.5 0.0 copy-start.2
  1.5 1.5 %reshape.10.v_ref = bf16[256,2048]{1,0:T(8,128)(2,1)S(1)} reshape(bf16[128,2,2048]{2,1,0:T(2,128)(2,1)} %param.7) | data formatting | bytes 2097152 | tf_op jit(solution)/shard_map/reshape | solution.py:323
  3.0 0.0 copy-done
  3.0 0.0 copy-done.1
  3.1 0.0 copy-done.2
  3.1 86.2 %shard_map.55 = bf16[128,2048]{1,0:T(8,128)(2,1)S(1)} custom-call(bf16[128,2048]{1,0:T(8,128)(2,1)S(1)} %copy-done, bf16[256,2048]{1,0:T(8,128)(2,1)S(1)} %reshape.9.k_ref, bf16[256,2048]{1,0:T(8,128)(2,1)S(1)} %reshape.10.v_ref, f32[2,16,128]{2,1,0:T(8,128)S(1)} %copy-done.1, f32[1,2048]{1,0:T(1,128)S(1)} %bitcast.1), custom_call_target="tpu_custom_call" | custom-call | tf_op jit(solution)/shard_map/pallas_call | solution.py:329
  89.2 0.8 copy.7
Async XLA Ops:
  1.5 1.6 %copy-start = (bf16[128,2048]{1,0:T(8,128)(2,1)S(1)}, bf16[128,2048]{1,0:T(8,128)(2,1)}, u32[]{:S(2)}) copy-start(bf16[128,2048]{1,0:T(8,128)(2,1)} %q_ref.1) | copy-start | bytes 1572868
  1.5 1.6 %copy-start.1 = (f32[2,16,128]{2,1,0:T(8,128)S(1)}, f32[2,16,128]{2,1,0:T(8,128)}, u32[]{:S(2)}) copy-start(f32[2,16,128]{2,1,0:T(8,128)} %b_ref.1) | copy-start | bytes 49156
  1.5 1.6 %copy-start.2 = (f32[2048]{0:T(1024)S(1)}, f32[2048]{0:T(1024)}, u32[]{:S(2)}) copy-start(f32[2048]{0:T(1024)} %param.9) | copy-start | bytes 24580

commit v5 on v4

--- a/solution.py
+++ b/solution.py
@@ -10,8 +10,6 @@
 F32 = jnp.float32
 BF16 = jnp.bfloat16
 MESH = pl.DeviceIdType.MESH
-GROUP = 4
-
 
 def dot(a, b):
     return lax.dot_general(a, b, (((1,), (0,)), ((), ())), preferred_element_type=F32)
@@ -68,9 +66,7 @@
     heads, size = maps.shape[0], maps.shape[1]
     count, rows = q_ref.shape[0], k_ref.shape[0]
     half = rows // 2
-    steps, group = beta_ref.shape[0], beta_ref.shape[2]
-    n_pairs, pairs_at_once = heads // 2, group // 2
-    span = group * size
+    n_pairs = heads // 2
     at, grp = lax.axis_index("inner"), lax.axis_index("outer")
     first, last = at == 0, at == n_in - 1
     has_prev = grp > 0
@@ -101,9 +97,9 @@
             part = strength.astype(BF16)
             strength = strength - part.astype(F32)
             spread = spread + dot_nt(pick, part)
-    for step in range(steps):
-        beta_ref[step] = spread[:, step * group : (step + 1) * group]
-    pl.semaphore_wait(barrier, sum(c.astype(jnp.int32) for c, _ in greetings))
+    for j in range(n_pairs):
+        beta_ref[j] = spread[:, 2 * j : 2 * j + 2]
+    peers = sum(c.astype(jnp.int32) for c, _ in greetings)
 
     def send_pre(h, fwd, src):
         return pltpu.make_async_remote_copy(
@@ -123,23 +119,23 @@
 
     row_h = lax.broadcasted_iota(jnp.int32, (half, half), 0)
     col_h = lax.broadcasted_iota(jnp.int32, (half, half), 1)
-    span_of = [slice(h * size, (h + 1) * size) for h in range(group)]
-
-    def lanes(step):
-        return pl.ds(pl.multiple_of(step * span, span), span)
-
-    def make_maps(step):
+
+    def lanes(pair, group):
+        return pl.ds(pl.multiple_of(pair * 2 * size, 2 * size), group * size)
+
+    def make_maps(pair, group):
+        span_of = [slice(h * size, (h + 1) * size) for h in range(group)]
         masks = [mask_ref[m] for m in range(mask_ref.shape[0])]
         strict = row_h > col_h
         eye = (row_h == col_h).astype(F32)
-        beta_all = beta_ref[step]
-        k_all, v_all = k_ref[:, lanes(step)], v_ref[:, lanes(step)]
+        beta_pairs = [beta_ref[pair + j] for j in range(group // 2)]
+        k_all, v_all = k_ref[:, lanes(pair, group)], v_ref[:, lanes(pair, group)]
         k = [k_all[:, c] for c in span_of]
         n00, n10, n11, rhs = [], [], [], []
         for h in range(group):
             kf = k[h].astype(F32)
             inv = 1.0 / (jnp.sum(kf * kf, axis=-1, keepdims=True) + 1e-06)
-            beta = beta_all[:, h : h + 1]
+            beta = beta_pairs[h // 2][:, h % 2 : h % 2 + 1]
             coef = beta * inv
             k0, k1 = k[h][:half], k[h][half:]
             n00.append(split(jnp.where(strict, coef[:half] * dot_nt(k0, k0), 0.0)))
@@ -161,28 +157,29 @@
             r = rhs[h][half:] - (dot(n10[h][0], th) + (dot(n10[h][1], th) + dot(n10[h][0], tl)))
             low.append(solve(inverse[group + h], n11[h], r))
         for h in range(group):
-            head = step * group + h
+            head = 2 * pair + h
             zh = jnp.concatenate([top[h][0], low[h][0]], axis=0)
             zl = jnp.concatenate([top[h][1], low[h][1]], axis=0)
             kz = dot_tn(k[h], zh) + dot_tn(k[h], zl)
             maps[head, :, :size] = eye - kz[:, size:]
             maps[head, :, size:] = kz[:, :size]
-            zhi[h] = zh
-            zlo[h] = zl
-
-    def make_outs(step):
+            zhi[head] = zh
+            zlo[head] = zl
+
+    def make_outs(pair, group):
+        span_of = [slice(h * size, (h + 1) * size) for h in range(group)]
         tok = lax.broadcasted_iota(jnp.int32, (count, rows), 0)
         virt = lax.broadcasted_iota(jnp.int32, (count, rows), 1)
         seen = virt <= 2 * tok + 1
-        k_all, q_all = k_ref[:, lanes(step)], q_ref[:, lanes(step)]
+        k_all, q_all = k_ref[:, lanes(pair, group)], q_ref[:, lanes(pair, group)]
         for h in range(group):
-            head = step * group + h
+            head = 2 * pair + h
             q = q_all[:, span_of[h]]
             qf = q.astype(F32)
             rq = lax.rsqrt(jnp.sum(qf * qf, axis=-1, keepdims=True) + 1e-06)
             ph, plo = split(jnp.where(seen, dot_nt(q, k_all[:, span_of[h]]), 0.0))
-            zh = zhi[h]
-            pz = dot(ph, zh) + (dot(plo, zh) + dot(ph, zlo[h]))
+            zh = zhi[head]
+            pz = dot(ph, zh) + (dot(plo, zh) + dot(ph, zlo[head]))
             outs[head, :, :size] = pz[:, :size] * rq
             outs[head, :, size:] = (qf - pz[:, size:]) * rq
 
@@ -209,23 +206,22 @@
     def advance(src, h):
         return dot3(src[h, :, :size], state[h]) + src[h, :, size:]
 
-    def enter(h, fwd):
-        end = last if fwd else first
-
-        @pl.when(end & has_prev)
+    def chain(h, fwd):
+        @pl.when(has_prev)
         def _():
             send_chain(h).wait_recv()
 
-        @pl.when(end & jnp.logical_not(has_prev))
+        @pl.when(jnp.logical_not(has_prev))
         def _():
             state[h] = jnp.zeros((size, size), F32)
 
-        @pl.when(end & has_next)
+        @pl.when(has_next)
         def _():
             after[h] = advance(comp, h)
             send_chain(h).start()
 
-        @pl.when(jnp.logical_not(end))
+    def hand(h, fwd):
+        @pl.when(jnp.logical_not(last if fwd else first))
         def _():
             send_relay(h, fwd).wait_recv()
 
@@ -246,12 +242,15 @@
         write(2 * j, advance(pre, 2 * j))
 
     back = n_in - 1 - at
-    shift = n_in + grp // 2
+    shift = grp // 2
     pairs = (
-        (0, True, jnp.where(first, 0, at + 1), shift + back),
-        (1, False, jnp.where(last, 0, back + 1), shift + at),
+        (0, True, jnp.where(first, 0, at + 1), last, back),
+        (1, False, jnp.where(last, 0, back + 1), first, at),
     )
-    leave = shift + n_in - 1
+
+    def handed(t):
+        early, late = t - n_in + 1, 2 * (t - n_pairs) + 2
+        return jnp.clip(jnp.minimum(early, late), 0, n_pairs)
 
     @pl.when(first)
     def _():
@@ -261,30 +260,51 @@
             pre[2 * j] = unit
 
     def sweep(t, _):
-        part = t % pairs_at_once
-
-        @pl.when((t < n_pairs) & (part == 0))
-        def _():
-            make_maps(t // pairs_at_once)
-
-        for off, fwd, skew, _ in pairs:
+        wide = (t % 2 == 0) & (t >= 2) & (t < n_pairs)
+
+        @pl.when(t < 2)
+        def _():
+            make_maps(t, 2)
+
+        @pl.when(wide)
+        def _():
+            make_maps(t, 4)
+
+        @pl.when(t == 0)
+        def _():
+            pl.semaphore_wait(barrier, peers)
+
+        for off, fwd, skew, _, _ in pairs:
             @pl.when((t >= skew) & (t < n_pairs + skew))
             def _():
                 prefix((t - skew) * 2 + off, fwd)
 
-        for off, fwd, _, skew in pairs:
-            @pl.when((t >= skew) & (t < n_pairs + skew))
-            def _():
-                enter((t - skew) * 2 + off, fwd)
-
-        @pl.when((t < n_pairs) & (part == pairs_at_once - 1))
-        def _():
-            make_outs(t // pairs_at_once)
-
-        @pl.when((t >= leave) & (t < n_pairs + leave))
-        def _():
-            emit(t - leave)
-
+        lead = t - n_in - shift
+        for off, fwd, _, end, _ in pairs:
+            @pl.when(end & (lead >= 0) & (lead < n_pairs))
+            def _():
+                chain(lead * 2 + off, fwd)
+
+        for off, fwd, _, _, hops in pairs:
+            now = t - shift - hops
+
+            def pass_on(j, _):
+                hand(2 * j + off, fwd)
+                return 0
+
+            lax.fori_loop(handed(now - 1), handed(now), pass_on, 0)
+
+        @pl.when((t % 2 == 1) & (t < n_pairs))
+        def _():
+            make_outs(t - 1, 4)
+
+        now = t - shift - (n_in - 1)
+
+        def leave(j, _):
+            emit(j)
+            return 0
+
+        lax.fori_loop(handed(now - 1), handed(now), leave, 0)
         return 0
 
     lax.fori_loop(0, n_pairs + 2 * n_in + n_out // 2, sweep, 0)
@@ -316,7 +336,6 @@
     heads = beta_logit.shape[1]
     size = width // heads
     rows = 2 * count
-    steps = heads // GROUP
     half = rows // 2
     n_in, n_out = lax.axis_size("inner"), lax.axis_size("outer")
     k2 = keys.reshape(rows, width)
@@ -325,7 +344,7 @@
     sems = pltpu.SemaphoreType.DMA((heads,))
     wide = pltpu.VMEM((heads, size, 2 * size), F32)
     square = pltpu.VMEM((heads, size, size), F32)
-    solved = pltpu.VMEM((GROUP, rows, 2 * size), BF16)
+    solved = pltpu.VMEM((heads, rows, 2 * size), BF16)
     return pl.pallas_call(
         functools.partial(layer_kernel, n_in, n_out),
         out_shape=jax.ShapeDtypeStruct((count, width), BF16),
@@ -333,7 +352,7 @@
         out_specs=vmem,
         scratch_shapes=[
             pltpu.VMEM((half.bit_length(), half, half), BF16),
-            pltpu.VMEM((steps, rows, GROUP), F32),
+            pltpu.VMEM((heads // 2, rows, 2), F32),
             wide, solved, solved,
             pltpu.VMEM((heads, count, 2 * size), F32),
             wide, wide, square, square, square,

time: 90.4 us -> 93.1 us (1.030)
  Pallas kernels: 86.2 us -> 89 us
    pallas_call x1, Pallas kernels: 86.2 us -> 89 us  [local(): pl.pallas_call(functools.partial(layer_kernel, n_in, n_out), out_shape=ja...]
where the time goes in v5:
time: 93.1 us; the launch traced here: 92.8 us
  Pallas kernels  89 us (96%)
  local copies, waits for them, and re-layouts  3.8 us (4%)
    pallas_call x1, Pallas kernels, local(): pl.pallas_call(functools.partial(layer_kernel, n_in, n_out), out_shape=ja...  89 us

profile of v5, /device:TPU:6, one launch (start us, length us, event | category | flops | bytes accessed | tf_op | source)
XLA Modules:
  0.0 92.8 jit_solution(3297775052829370535)
XLA Ops:
  0.0 1.5 %reshape.9.k_ref = bf16[256,2048]{1,0:T(8,128)(2,1)S(1)} reshape(bf16[128,2,2048]{2,1,0:T(2,128)(2,1)} %param.6) | data formatting | bytes 2097152 | tf_op jit(solution)/shard_map/reshape | solution.py:341
  1.5 0.0 copy-start
  1.5 0.0 copy-start.1
  1.5 0.0 copy-start.2
  1.5 1.5 %reshape.10.v_ref = bf16[256,2048]{1,0:T(8,128)(2,1)S(1)} reshape(bf16[128,2,2048]{2,1,0:T(2,128)(2,1)} %param.7) | data formatting | bytes 2097152 | tf_op jit(solution)/shard_map/reshape | solution.py:342
  3.0 0.0 copy-done
  3.0 0.0 copy-done.1
  3.1 0.0 copy-done.2
  3.1 89.0 %shard_map.55 = bf16[128,2048]{1,0:T(8,128)(2,1)S(1)} custom-call(bf16[128,2048]{1,0:T(8,128)(2,1)S(1)} %copy-done, bf16[256,2048]{1,0:T(8,128)(2,1)S(1)} %reshape.9.k_ref, bf16[256,2048]{1,0:T(8,128)(2,1)S(1)} %reshape.10.v_ref, f32[2,16,128]{2,1,0:T(8,128)S(1)} %copy-done.1, f32[1,2048]{1,0:T(1,128)S(1)} %bitcast.1), custom_call_target="tpu_custom_call" | custom-call | tf_op jit(solution)/shard_map/pallas_call | solution.py:348
  92.0 0.8 copy.7
Async XLA Ops:
  1.5 1.6 %copy-start = (bf16[128,2048]{1,0:T(8,128)(2,1)S(1)}, bf16[128,2048]{1,0:T(8,128)(2,1)}, u32[]{:S(2)}) copy-start(bf16[128,2048]{1,0:T(8,128)(2,1)} %q_ref.1) | copy-start | bytes 1572868
  1.5 1.6 %copy-start.1 = (f32[2,16,128]{2,1,0:T(8,128)S(1)}, f32[2,16,128]{2,1,0:T(8,128)}, u32[]{:S(2)}) copy-start(f32[2,16,128]{2,1,0:T(8,128)} %b_ref.1) | copy-start | bytes 49156
  1.5 1.6 %copy-start.2 = (f32[2048]{0:T(1024)S(1)}, f32[2048]{0:T(1024)}, u32[]{:S(2)}) copy-start(f32[2048]{0:T(1024)} %param.9) | copy-start | bytes 24580

commit v6 on v4

--- a/solution.py
+++ b/solution.py
@@ -103,7 +103,7 @@
             spread = spread + dot_nt(pick, part)
     for step in range(steps):
         beta_ref[step] = spread[:, step * group : (step + 1) * group]
-    pl.semaphore_wait(barrier, sum(c.astype(jnp.int32) for c, _ in greetings))
+    peers = sum(c.astype(jnp.int32) for c, _ in greetings)
 
     def send_pre(h, fwd, src):
         return pltpu.make_async_remote_copy(
@@ -246,10 +246,10 @@
         write(2 * j, advance(pre, 2 * j))
 
     back = n_in - 1 - at
-    shift = n_in + grp // 2
+    shift = 2 * (n_in - 1) + grp // 2
     pairs = (
-        (0, True, jnp.where(first, 0, at + 1), shift + back),
-        (1, False, jnp.where(last, 0, back + 1), shift + at),
+        (0, True, 2 * at, shift + back),
+        (1, False, 2 * back, shift + at),
     )
     leave = shift + n_in - 1
 
@@ -267,6 +267,10 @@
         def _():
             make_maps(t // pairs_at_once)
 
+        @pl.when(t == 0)
+        def _():
+            pl.semaphore_wait(barrier, peers)
+
         for off, fwd, skew, _ in pairs:
             @pl.when((t >= skew) & (t < n_pairs + skew))
             def _():
@@ -287,7 +291,7 @@
 
         return 0
 
-    lax.fori_loop(0, n_pairs + 2 * n_in + n_out // 2, sweep, 0)
+    lax.fori_loop(0, n_pairs + 3 * n_in + n_out // 2, sweep, 0)
 
     def drain(j, _):
         for fwd in (True, False):

time: 90.4 us -> 84.2 us (0.931)
  Pallas kernels: 86.2 us -> 79.7 us
    pallas_call x1, Pallas kernels: 86.2 us -> 79.7 us  [local(): pl.pallas_call(functools.partial(layer_kernel, n_in, n_out), out_shape=ja...]
where the time goes in v6:
time: 84.2 us; the launch traced here: 83.6 us
  Pallas kernels  79.7 us (95%)
  local copies, waits for them, and re-layouts  3.8 us (5%)
    pallas_call x1, Pallas kernels, local(): pl.pallas_call(functools.partial(layer_kernel, n_in, n_out), out_shape=ja...  79.7 us

profile of v6, /device:TPU:6, one launch (start us, length us, event | category | flops | bytes accessed | tf_op | source)
XLA Modules:
  0.0 83.6 jit_solution(8405854287708972597)
XLA Ops:
  0.0 1.5 %reshape.9.k_ref = bf16[256,2048]{1,0:T(8,128)(2,1)S(1)} reshape(bf16[128,2,2048]{2,1,0:T(2,128)(2,1)} %param.6) | data formatting | bytes 2097152 | tf_op jit(solution)/shard_map/reshape | solution.py:326
  1.5 0.0 copy-start
  1.5 0.0 copy-start.1
  1.5 0.0 copy-start.2
  1.5 1.5 %reshape.10.v_ref = bf16[256,2048]{1,0:T(8,128)(2,1)S(1)} reshape(bf16[128,2,2048]{2,1,0:T(2,128)(2,1)} %param.7) | data formatting | bytes 2097152 | tf_op jit(solution)/shard_map/reshape | solution.py:327
  3.0 0.0 copy-done
  3.0 0.0 copy-done.1
  3.1 0.0 copy-done.2
  3.1 79.7 %shard_map.55 = bf16[128,2048]{1,0:T(8,128)(2,1)S(1)} custom-call(bf16[128,2048]{1,0:T(8,128)(2,1)S(1)} %copy-done, bf16[256,2048]{1,0:T(8,128)(2,1)S(1)} %reshape.9.k_ref, bf16[256,2048]{1,0:T(8,128)(2,1)S(1)} %reshape.10.v_ref, f32[2,16,128]{2,1,0:T(8,128)S(1)} %copy-done.1, f32[1,2048]{1,0:T(1,128)S(1)} %bitcast.1), custom_call_target="tpu_custom_call" | custom-call | tf_op jit(solution)/shard_map/pallas_call | solution.py:333
  82.8 0.8 copy.7
Async XLA Ops:
  1.5 1.6 %copy-start = (bf16[128,2048]{1,0:T(8,128)(2,1)S(1)}, bf16[128,2048]{1,0:T(8,128)(2,1)}, u32[]{:S(2)}) copy-start(bf16[128,2048]{1,0:T(8,128)(2,1)} %q_ref.1) | copy-start | bytes 1572868
  1.5 1.6 %copy-start.1 = (f32[2,16,128]{2,1,0:T(8,128)S(1)}, f32[2,16,128]{2,1,0:T(8,128)}, u32[]{:S(2)}) copy-start(f32[2,16,128]{2,1,0:T(8,128)} %b_ref.1) | copy-start | bytes 49156
  1.5 1.6 %copy-start.2 = (f32[2048]{0:T(1024)S(1)}, f32[2048]{0:T(1024)}, u32[]{:S(2)}) copy-start(f32[2048]{0:T(1024)} %param.9) | copy-start | bytes 24580

commit v7 on v6

--- a/solution.py
+++ b/solution.py
@@ -30,10 +30,12 @@
     return hi, (x - hi.astype(F32)).astype(BF16)
 
 
+def dot3_split(a, b):
+    return dot(a[0], b[0]) + (dot(a[0], b[1]) + dot(a[1], b[0]))
+
+
 def dot3(a, b):
-    ah, al = split(a)
-    bh, bl = split(b)
-    return dot(ah, bh) + (dot(ah, bl) + dot(al, bh))
+    return dot3_split(split(a), split(b))
 
 
 def unit_lower_inverses(systems, masks):
@@ -105,9 +107,12 @@
         beta_ref[step] = spread[:, step * group : (step + 1) * group]
     peers = sum(c.astype(jnp.int32) for c, _ in greetings)
 
-    def send_pre(h, fwd, src):
+    parts = (slice(0, size), slice(size, 2 * size))
+
+    def send_pre(h, fwd, src, piece):
         return pltpu.make_async_remote_copy(
-            src.at[h], pre.at[h], s_pre.at[h], r_pre.at[h],
+            src.at[h, :, parts[piece]], pre.at[h, :, parts[piece]],
+            s_pre.at[h, piece], r_pre.at[h, piece],
             device_id=(grp, at + 1 if fwd else at - 1), device_id_type=MESH)
 
     def send_chain(h):
@@ -191,20 +196,29 @@
 
         @pl.when(start)
         def _():
-            send_pre(h, fwd, maps).start()
+            send_pre(h, fwd, maps, 0).start()
+            send_pre(h, fwd, maps, 1).start()
 
         @pl.when(jnp.logical_not(start))
         def _():
-            send_pre(h, fwd, comp).wait_recv()
-            own, got = maps[h], pre[h]
-            late, early = (own, got) if fwd else (got, own)
-            both = dot3(late[:, :size], early)
-            comp[h, :, :size] = both[:, :size]
-            comp[h, :, size:] = both[:, size:] + late[:, size:]
+            own_a, own_b = split(maps[h, :, :size]), maps[h, :, size:]
+            send_pre(h, fwd, comp, 0).wait_recv()
+            got_a = split(pre[h, :, :size])
+            late, early = (own_a, got_a) if fwd else (got_a, own_a)
+            comp[h, :, :size] = dot3_split(late, early)
 
             @pl.when(jnp.logical_not(end))
             def _():
-                send_pre(h, fwd, comp).start()
+                send_pre(h, fwd, comp, 0).start()
+
+            send_pre(h, fwd, comp, 1).wait_recv()
+            got_b = pre[h, :, size:]
+            late_b, early_b = (own_b, got_b) if fwd else (got_b, own_b)
+            comp[h, :, size:] = dot3_split(late, split(early_b)) + late_b
+
+            @pl.when(jnp.logical_not(end))
+            def _():
+                send_pre(h, fwd, comp, 1).start()
 
     def advance(src, h):
         return dot3(src[h, :, :size], state[h]) + src[h, :, size:]
@@ -248,10 +262,10 @@
     back = n_in - 1 - at
     shift = 2 * (n_in - 1) + grp // 2
     pairs = (
-        (0, True, 2 * at, shift + back),
-        (1, False, 2 * back, shift + at),
+        (0, True, 2 * at, shift + 2 * back),
+        (1, False, 2 * back, shift + 2 * at),
     )
-    leave = shift + n_in - 1
+    leave = shift + 2 * (n_in - 1)
 
     @pl.when(first)
     def _():
@@ -291,7 +305,7 @@
 
         return 0
 
-    lax.fori_loop(0, n_pairs + 3 * n_in + n_out // 2, sweep, 0)
+    lax.fori_loop(0, n_pairs + 4 * n_in + n_out // 2, sweep, 0)
 
     def drain(j, _):
         for fwd in (True, False):
@@ -300,7 +314,8 @@
 
             @pl.when(jnp.logical_not(end))
             def _():
-                send_pre(h, fwd, comp).wait_send()
+                send_pre(h, fwd, comp, 0).wait_send()
+                send_pre(h, fwd, comp, 1).wait_send()
 
             @pl.when(end & has_next)
             def _():
@@ -327,6 +342,7 @@
     v2 = values.reshape(rows, width)
     vmem = pl.BlockSpec(memory_space=pltpu.VMEM)
     sems = pltpu.SemaphoreType.DMA((heads,))
+    sems2 = pltpu.SemaphoreType.DMA((heads, 2))
     wide = pltpu.VMEM((heads, size, 2 * size), F32)
     square = pltpu.VMEM((heads, size, size), F32)
     solved = pltpu.VMEM((GROUP, rows, 2 * size), BF16)
@@ -341,7 +357,7 @@
             wide, solved, solved,
             pltpu.VMEM((heads, count, 2 * size), F32),
             wide, wide, square, square, square,
-            sems, sems, sems, sems, sems,
+            sems2, sems2, sems, sems, sems,
         ],
         compiler_params=pltpu.CompilerParams(
             collective_id=0, has_side_effects=True, vmem_limit_bytes=48 * 1024 * 1024

time: 84.2 us -> 80.5 us (0.956)
  Pallas kernels: 79.7 us -> 76.5 us
    pallas_call x1, Pallas kernels: 79.7 us -> 76.5 us  [local(): pl.pallas_call(functools.partial(layer_kernel, n_in, n_out), out_shape=ja...]
where the time goes in v7:
time: 80.5 us; the launch traced here: 80.4 us
  Pallas kernels  76.5 us (95%)
  local copies, waits for them, and re-layouts  3.8 us (5%)
    pallas_call x1, Pallas kernels, local(): pl.pallas_call(functools.partial(layer_kernel, n_in, n_out), out_shape=ja...  76.5 us

profile of v7, /device:TPU:6, one launch (start us, length us, event | category | flops | bytes accessed | tf_op | source)
XLA Modules:
  0.0 80.4 jit_solution(16135946886447055508)
XLA Ops:
  0.0 1.5 %reshape.9.k_ref = bf16[256,2048]{1,0:T(8,128)(2,1)S(1)} reshape(bf16[128,2,2048]{2,1,0:T(2,128)(2,1)} %param.6) | data formatting | bytes 2097152 | tf_op jit(solution)/shard_map/reshape | solution.py:341
  1.5 0.0 copy-start
  1.5 0.0 copy-start.1
  1.5 0.0 copy-start.2
  1.5 1.5 %reshape.10.v_ref = bf16[256,2048]{1,0:T(8,128)(2,1)S(1)} reshape(bf16[128,2,2048]{2,1,0:T(2,128)(2,1)} %param.7) | data formatting | bytes 2097152 | tf_op jit(solution)/shard_map/reshape | solution.py:342
  3.0 0.0 copy-done
  3.0 0.0 copy-done.1
  3.1 0.0 copy-done.2
  3.1 76.5 %shard_map.55 = bf16[128,2048]{1,0:T(8,128)(2,1)S(1)} custom-call(bf16[128,2048]{1,0:T(8,128)(2,1)S(1)} %copy-done, bf16[256,2048]{1,0:T(8,128)(2,1)S(1)} %reshape.9.k_ref, bf16[256,2048]{1,0:T(8,128)(2,1)S(1)} %reshape.10.v_ref, f32[2,16,128]{2,1,0:T(8,128)S(1)} %copy-done.1, f32[1,2048]{1,0:T(1,128)S(1)} %bitcast.1), custom_call_target="tpu_custom_call" | custom-call | tf_op jit(solution)/shard_map/pallas_call | solution.py:349
  79.6 0.8 copy.7
Async XLA Ops:
  1.5 1.6 %copy-start = (bf16[128,2048]{1,0:T(8,128)(2,1)S(1)}, bf16[128,2048]{1,0:T(8,128)(2,1)}, u32[]{:S(2)}) copy-start(bf16[128,2048]{1,0:T(8,128)(2,1)} %q_ref.1) | copy-start | bytes 1572868
  1.5 1.6 %copy-start.1 = (f32[2,16,128]{2,1,0:T(8,128)S(1)}, f32[2,16,128]{2,1,0:T(8,128)}, u32[]{:S(2)}) copy-start(f32[2,16,128]{2,1,0:T(8,128)} %b_ref.1) | copy-start | bytes 49156
  1.5 1.6 %copy-start.2 = (f32[2048]{0:T(1024)S(1)}, f32[2048]{0:T(1024)}, u32[]{:S(2)}) copy-start(f32[2048]{0:T(1024)} %param.9) | copy-start | bytes 24580

commit v8 on v7

--- a/solution.py
+++ b/solution.py
@@ -10,7 +10,6 @@
 F32 = jnp.float32
 BF16 = jnp.bfloat16
 MESH = pl.DeviceIdType.MESH
-GROUP = 4
 
 
 def dot(a, b):
@@ -70,9 +69,7 @@
     heads, size = maps.shape[0], maps.shape[1]
     count, rows = q_ref.shape[0], k_ref.shape[0]
     half = rows // 2
-    steps, group = beta_ref.shape[0], beta_ref.shape[2]
-    n_pairs, pairs_at_once = heads // 2, group // 2
-    span = group * size
+    n_pairs = heads // 2
     at, grp = lax.axis_index("inner"), lax.axis_index("outer")
     first, last = at == 0, at == n_in - 1
     has_prev = grp > 0
@@ -103,8 +100,8 @@
             part = strength.astype(BF16)
             strength = strength - part.astype(F32)
             spread = spread + dot_nt(pick, part)
-    for step in range(steps):
-        beta_ref[step] = spread[:, step * group : (step + 1) * group]
+    for j in range(n_pairs):
+        beta_ref[j] = spread[:, 2 * j : 2 * j + 2]
     peers = sum(c.astype(jnp.int32) for c, _ in greetings)
 
     parts = (slice(0, size), slice(size, 2 * size))
@@ -128,23 +125,23 @@
 
     row_h = lax.broadcasted_iota(jnp.int32, (half, half), 0)
     col_h = lax.broadcasted_iota(jnp.int32, (half, half), 1)
-    span_of = [slice(h * size, (h + 1) * size) for h in range(group)]
-
-    def lanes(step):
-        return pl.ds(pl.multiple_of(step * span, span), span)
-
-    def make_maps(step):
+
+    def lanes(pair, group):
+        return pl.ds(pl.multiple_of(pair * 2 * size, 2 * size), group * size)
+
+    def make_maps(pair, group):
+        span_of = [slice(h * size, (h + 1) * size) for h in range(group)]
         masks = [mask_ref[m] for m in range(mask_ref.shape[0])]
         strict = row_h > col_h
         eye = (row_h == col_h).astype(F32)
-        beta_all = beta_ref[step]
-        k_all, v_all = k_ref[:, lanes(step)], v_ref[:, lanes(step)]
+        beta_pairs = [beta_ref[pair + j] for j in range(group // 2)]
+        k_all, v_all = k_ref[:, lanes(pair, group)], v_ref[:, lanes(pair, group)]
         k = [k_all[:, c] for c in span_of]
         n00, n10, n11, rhs = [], [], [], []
         for h in range(group):
             kf = k[h].astype(F32)
             inv = 1.0 / (jnp.sum(kf * kf, axis=-1, keepdims=True) + 1e-06)
-            beta = beta_all[:, h : h + 1]
+            beta = beta_pairs[h // 2][:, h % 2 : h % 2 + 1]
             coef = beta * inv
             k0, k1 = k[h][:half], k[h][half:]
             n00.append(split(jnp.where(strict, coef[:half] * dot_nt(k0, k0), 0.0)))
@@ -166,28 +163,29 @@
             r = rhs[h][half:] - (dot(n10[h][0], th) + (dot(n10[h][1], th) + dot(n10[h][0], tl)))
             low.append(solve(inverse[group + h], n11[h], r))
         for h in range(group):
-            head = step * group + h
+            head = 2 * pair + h
             zh = jnp.concatenate([top[h][0], low[h][0]], axis=0)
             zl = jnp.concatenate([top[h][1], low[h][1]], axis=0)
             kz = dot_tn(k[h], zh) + dot_tn(k[h], zl)
             maps[head, :, :size] = eye - kz[:, size:]
             maps[head, :, size:] = kz[:, :size]
-            zhi[h] = zh
-            zlo[h] = zl
-
-    def make_outs(step):
+            zhi[head] = zh
+            zlo[head] = zl
+
+    def make_outs(pair, group):
+        span_of = [slice(h * size, (h + 1) * size) for h in range(group)]
         tok = lax.broadcasted_iota(jnp.int32, (count, rows), 0)
         virt = lax.broadcasted_iota(jnp.int32, (count, rows), 1)
         seen = virt <= 2 * tok + 1
-        k_all, q_all = k_ref[:, lanes(step)], q_ref[:, lanes(step)]
+        k_all, q_all = k_ref[:, lanes(pair, group)], q_ref[:, lanes(pair, group)]
         for h in range(group):
-            head = step * group + h
+            head = 2 * pair + h
             q = q_all[:, span_of[h]]
             qf = q.astype(F32)
             rq = lax.rsqrt(jnp.sum(qf * qf, axis=-1, keepdims=True) + 1e-06)
             ph, plo = split(jnp.where(seen, dot_nt(q, k_all[:, span_of[h]]), 0.0))
-            zh = zhi[h]
-            pz = dot(ph, zh) + (dot(plo, zh) + dot(ph, zlo[h]))
+            zh = zhi[head]
+            pz = dot(ph, zh) + (dot(plo, zh) + dot(ph, zlo[head]))
             outs[head, :, :size] = pz[:, :size] * rq
             outs[head, :, size:] = (qf - pz[:, size:]) * rq
 
@@ -275,11 +273,13 @@
             pre[2 * j] = unit
 
     def sweep(t, _):
-        part = t % pairs_at_once
-
-        @pl.when((t < n_pairs) & (part == 0))
-        def _():
-            make_maps(t // pairs_at_once)
+        @pl.when(t < 2)
+        def _():
+            make_maps(t, 2)
+
+        @pl.when((t % 2 == 0) & (t >= 2) & (t < n_pairs))
+        def _():
+            make_maps(t, 4)
 
         @pl.when(t == 0)
         def _():
@@ -295,9 +295,9 @@
             def _():
                 enter((t - skew) * 2 + off, fwd)
 
-        @pl.when((t < n_pairs) & (part == pairs_at_once - 1))
-        def _():
-            make_outs(t // pairs_at_once)
+        @pl.when((t % 2 == 1) & (t < n_pairs))
+        def _():
+            make_outs(t - 1, 4)
 
         @pl.when((t >= leave) & (t < n_pairs + leave))
         def _():
@@ -335,7 +335,6 @@
     heads = beta_logit.shape[1]
     size = width // heads
     rows = 2 * count
-    steps = heads // GROUP
     half = rows // 2
     n_in, n_out = lax.axis_size("inner"), lax.axis_size("outer")
     k2 = keys.reshape(rows, width)
@@ -345,7 +344,7 @@
     sems2 = pltpu.SemaphoreType.DMA((heads, 2))
     wide = pltpu.VMEM((heads, size, 2 * size), F32)
     square = pltpu.VMEM((heads, size, size), F32)
-    solved = pltpu.VMEM((GROUP, rows, 2 * size), BF16)
+    solved = pltpu.VMEM((heads, rows, 2 * size), BF16)
     return pl.pallas_call(
         functools.partial(layer_kernel, n_in, n_out),
         out_shape=jax.ShapeDtypeStruct((count, width), BF16),
@@ -353,7 +352,7 @@
         out_specs=vmem,
         scratch_shapes=[
             pltpu.VMEM((half.bit_length(), half, half), BF16),
-            pltpu.VMEM((steps, rows, GROUP), F32),
+            pltpu.VMEM((heads // 2, rows, 2), F32),
             wide, solved, solved,
             pltpu.VMEM((heads, count, 2 * size), F32),
             wide, wide, square, square, square,

time: 80.5 us -> 82.5 us (1.025)
  Pallas kernels: 76.5 us -> 78.5 us
    pallas_call x1, Pallas kernels: 76.5 us -> 78.5 us  [local(): pl.pallas_call(functools.partial(layer_kernel, n_in, n_out), out_shape=ja...]
where the time goes in v8:
time: 82.5 us; the launch traced here: 82.4 us
  Pallas kernels  78.5 us (95%)
  local copies, waits for them, and re-layouts  3.8 us (5%)
    pallas_call x1, Pallas kernels, local(): pl.pallas_call(functools.partial(layer_kernel, n_in, n_out), out_shape=ja...  78.5 us

profile of v8, /device:TPU:6, one launch (start us, length us, event | category | flops | bytes accessed | tf_op | source)
XLA Modules:
  0.0 82.4 jit_solution(8641773030072024627)
XLA Ops:
  0.0 1.5 %reshape.9.k_ref = bf16[256,2048]{1,0:T(8,128)(2,1)S(1)} reshape(bf16[128,2,2048]{2,1,0:T(2,128)(2,1)} %param.6) | data formatting | bytes 2097152 | tf_op jit(solution)/shard_map/reshape | solution.py:340
  1.5 0.0 copy-start
  1.5 0.0 copy-start.1
  1.5 0.0 copy-start.2
  1.5 1.5 %reshape.10.v_ref = bf16[256,2048]{1,0:T(8,128)(2,1)S(1)} reshape(bf16[128,2,2048]{2,1,0:T(2,128)(2,1)} %param.7) | data formatting | bytes 2097152 | tf_op jit(solution)/shard_map/reshape | solution.py:341
  3.0 0.0 copy-done
  3.0 0.0 copy-done.1
  3.1 0.0 copy-done.2
  3.1 78.5 %shard_map.55 = bf16[128,2048]{1,0:T(8,128)(2,1)S(1)} custom-call(bf16[128,2048]{1,0:T(8,128)(2,1)S(1)} %copy-done, bf16[256,2048]{1,0:T(8,128)(2,1)S(1)} %reshape.9.k_ref, bf16[256,2048]{1,0:T(8,128)(2,1)S(1)} %reshape.10.v_ref, f32[2,16,128]{2,1,0:T(8,128)S(1)} %copy-done.1, f32[1,2048]{1,0:T(1,128)S(1)} %bitcast.1), custom_call_target="tpu_custom_call" | custom-call | tf_op jit(solution)/shard_map/pallas_call | solution.py:348
  81.6 0.8 copy.7
Async XLA Ops:
  1.5 1.6 %copy-start = (bf16[128,2048]{1,0:T(8,128)(2,1)S(1)}, bf16[128,2048]{1,0:T(8,128)(2,1)}, u32[]{:S(2)}) copy-start(bf16[128,2048]{1,0:T(8,128)(2,1)} %q_ref.1) | copy-start | bytes 1572868
  1.5 1.6 %copy-start.1 = (f32[2,16,128]{2,1,0:T(8,128)S(1)}, f32[2,16,128]{2,1,0:T(8,128)}, u32[]{:S(2)}) copy-start(f32[2,16,128]{2,1,0:T(8,128)} %b_ref.1) | copy-start | bytes 49156
  1.5 1.6 %copy-start.2 = (f32[2048]{0:T(1024)S(1)}, f32[2048]{0:T(1024)}, u32[]{:S(2)}) copy-start(f32[2048]{0:T(1024)} %param.9) | copy-start | bytes 24580

commit v9 on v7

--- a/solution.py
+++ b/solution.py
@@ -172,8 +172,8 @@
             kz = dot_tn(k[h], zh) + dot_tn(k[h], zl)
             maps[head, :, :size] = eye - kz[:, size:]
             maps[head, :, size:] = kz[:, :size]
-            zhi[h] = zh
-            zlo[h] = zl
+            zhi[head] = zh
+            zlo[head] = zl
 
     def make_outs(step):
         tok = lax.broadcasted_iota(jnp.int32, (count, rows), 0)
@@ -186,8 +186,8 @@
             qf = q.astype(F32)
             rq = lax.rsqrt(jnp.sum(qf * qf, axis=-1, keepdims=True) + 1e-06)
             ph, plo = split(jnp.where(seen, dot_nt(q, k_all[:, span_of[h]]), 0.0))
-            zh = zhi[h]
-            pz = dot(ph, zh) + (dot(plo, zh) + dot(ph, zlo[h]))
+            zh = zhi[head]
+            pz = dot(ph, zh) + (dot(plo, zh) + dot(ph, zlo[head]))
             outs[head, :, :size] = pz[:, :size] * rq
             outs[head, :, size:] = (qf - pz[:, size:]) * rq
 
@@ -295,9 +295,9 @@
             def _():
                 enter((t - skew) * 2 + off, fwd)
 
-        @pl.when((t < n_pairs) & (part == pairs_at_once - 1))
-        def _():
-            make_outs(t // pairs_at_once)
+        @pl.when((t >= n_pairs) & (t < n_pairs + steps))
+        def _():
+            make_outs(t - n_pairs)
 
         @pl.when((t >= leave) & (t < n_pairs + leave))
         def _():
@@ -345,7 +345,7 @@
     sems2 = pltpu.SemaphoreType.DMA((heads, 2))
     wide = pltpu.VMEM((heads, size, 2 * size), F32)
     square = pltpu.VMEM((heads, size, size), F32)
-    solved = pltpu.VMEM((GROUP, rows, 2 * size), BF16)
+    solved = pltpu.VMEM((heads, rows, 2 * size), BF16)
     return pl.pallas_call(
         functools.partial(layer_kernel, n_in, n_out),
         out_shape=jax.ShapeDtypeStruct((count, width), BF16),

time: 80.5 us -> 79 us (0.981)
  Pallas kernels: 76.5 us -> 75 us
    pallas_call x1, Pallas kernels: 76.5 us -> 75 us  [local(): pl.pallas_call(functools.partial(layer_kernel, n_in, n_out), out_shape=ja...]
where the time goes in v9:
time: 79 us; the launch traced here: 78.8 us
  Pallas kernels  75 us (95%)
  local copies, waits for them, and re-layouts  3.8 us (5%)
    pallas_call x1, Pallas kernels, local(): pl.pallas_call(functools.partial(layer_kernel, n_in, n_out), out_shape=ja...  75 us

profile of v9, /device:TPU:6, one launch (start us, length us, event | category | flops | bytes accessed | tf_op | source)
XLA Modules:
  0.0 78.8 jit_solution(17824098156762654115)
XLA Ops:
  0.0 1.5 %reshape.9.k_ref = bf16[256,2048]{1,0:T(8,128)(2,1)S(1)} reshape(bf16[128,2,2048]{2,1,0:T(2,128)(2,1)} %param.6) | data formatting | bytes 2097152 | tf_op jit(solution)/shard_map/reshape | solution.py:341
  1.5 0.0 copy-start
  1.5 0.0 copy-start.1
  1.5 0.0 copy-start.2
  1.5 1.5 %reshape.10.v_ref = bf16[256,2048]{1,0:T(8,128)(2,1)S(1)} reshape(bf16[128,2,2048]{2,1,0:T(2,128)(2,1)} %param.7) | data formatting | bytes 2097152 | tf_op jit(solution)/shard_map/reshape | solution.py:342
  3.0 0.0 copy-done
  3.0 0.0 copy-done.1
  3.1 0.0 copy-done.2
  3.1 75.0 %shard_map.55 = bf16[128,2048]{1,0:T(8,128)(2,1)S(1)} custom-call(bf16[128,2048]{1,0:T(8,128)(2,1)S(1)} %copy-done, bf16[256,2048]{1,0:T(8,128)(2,1)S(1)} %reshape.9.k_ref, bf16[256,2048]{1,0:T(8,128)(2,1)S(1)} %reshape.10.v_ref, f32[2,16,128]{2,1,0:T(8,128)S(1)} %copy-done.1, f32[1,2048]{1,0:T(1,128)S(1)} %bitcast.1), custom_call_target="tpu_custom_call" | custom-call | tf_op jit(solution)/shard_map/pallas_call | solution.py:349
  78.0 0.8 %copy.7 = bf16[128,2048]{1,0:T(8,128)(2,1)} copy(bf16[128,2048]{1,0:T(8,128)(2,1)S(1)} %shard_map.55) | data formatting | bytes 1048576
Async XLA Ops:
  1.5 1.6 %copy-start = (bf16[128,2048]{1,0:T(8,128)(2,1)S(1)}, bf16[128,2048]{1,0:T(8,128)(2,1)}, u32[]{:S(2)}) copy-start(bf16[128,2048]{1,0:T(8,128)(2,1)} %q_ref.1) | copy-start | bytes 1572868
  1.5 1.6 %copy-start.1 = (f32[2,16,128]{2,1,0:T(8,128)S(1)}, f32[2,16,128]{2,1,0:T(8,128)}, u32[]{:S(2)}) copy-start(f32[2,16,128]{2,1,0:T(8,128)} %b_ref.1) | copy-start | bytes 49156
  1.5 1.6 %copy-start.2 = (f32[2048]{0:T(1024)S(1)}, f32[2048]{0:T(1024)}, u32[]{:S(2)}) copy-start(f32[2048]{0:T(1024)} %param.9) | copy-start | bytes 24580
